TPU v7x, 32 devices: a whole 2x2x4 slice. The times are simulated.
32 devices in a mesh: dom: 8 (over z, x), cls: 4 (over y, core).
Axes of the slice: x: 2, y: 2, z: 4, core: 2. Of those that a mesh axis runs over, the one named last changes fastest.
Arguments:
- particles: bfloat16 [256, 128, 9, 128], P(None, ('dom', 'cls')), may hold values from -6 to 6
- references: bfloat16 [256, 200, 128], P(None, 'cls'), may hold values from -6 to 6
- class_ids: int32 [128, 3], P(('dom', 'cls')), may hold values from 0 to 199, all different within a row
- counts: int32 [128], P(('dom', 'cls')), may hold values from 1 to 3
- shift_ids: int32 [128, 3], P(('dom', 'cls')), may hold values from 0 to 8
- weights: bfloat16 [128, 3], P(('dom', 'cls')), may hold values from 0.049804688 to 1
Outputs:
- best_scores: float32 [128, 200], P('dom', 'cls')
- class_means: float32 [256, 200, 128], P('dom', 'cls')
Inputs may be any that keep to these rules, and one draw needn't show every extreme that they name: `class_ids`: each particle's row names 3 different classes and every class is named by some row; only the first counts entries of a row are significant.
All inputs are finite; a program needn't handle non-finite values.
Results may differ from a plain program's by a relative error of at most 0.0012.
Values may be sent and summed in bfloat16 or wider, within the bound.
A program may use at most 128 MiB of HBM per device.

v0:
```python
import math

import jax
import jax.numpy as jnp
from jax import lax
from jax.sharding import PartitionSpec as P


def angle_table(angles):
    harmonic = jnp.arange(angles, dtype=jnp.int32)
    product = harmonic[:, None] * harmonic[None, :] % angles
    phase_angle = product.astype(jnp.float32) * (2.0 * math.pi / angles)
    return jnp.stack([jnp.cos(phase_angle), -jnp.sin(phase_angle)]).astype(jnp.bfloat16)


def real_form(references, cycles):
    real_part = references[:, :, :cycles]
    imag_part = references[:, :, cycles:]
    swapped = jnp.concatenate([-imag_part, real_part], axis=2)
    return jnp.concatenate([references, swapped], axis=1)


def on_device(particles, references, class_ids, counts, shift_ids, weights):
    dom_size = lax.axis_size("dom")
    cls_index = lax.axis_index("cls")
    angles = references.shape[0]
    class_count = references.shape[1]
    cycle_parts = references.shape[2]
    cycles = cycle_parts // 2
    shifts = particles.shape[2]
    list_length = class_ids.shape[1]
    all_images, all_ids, all_counts, all_shifts, all_weights = (
        lax.all_gather(particles, "cls", axis=1, tiled=True),
        lax.all_gather(class_ids, "cls", axis=0, tiled=True),
        lax.all_gather(counts, "cls", axis=0, tiled=True),
        lax.all_gather(shift_ids, "cls", axis=0, tiled=True),
        lax.all_gather(weights, "cls", axis=0, tiled=True),
    )
    group_rows = all_images.shape[1]
    table_rows = angle_table(angles)
    stacked = real_form(references, cycles)
    scale = 1.0 / math.sqrt(2.0 * cycles * angles)
    block_rows_each = 4

    def score_block(block_index):
        block = lax.dynamic_slice_in_dim(
            all_images, block_index * block_rows_each, block_rows_each, 1
        )
        flat_block = block.reshape(angles, block_rows_each * shifts, cycle_parts)
        products = jnp.einsum(
            "mnc,mqc->mnq", flat_block, stacked, preferred_element_type=jnp.float32
        )
        rounded = products.astype(jnp.bfloat16).reshape(
            angles, block_rows_each * shifts, 2, class_count
        )
        scores = jnp.einsum(
            "mnk,mp->nkp", rounded[:, :, 0], table_rows[0], preferred_element_type=jnp.float32
        )
        scores = scores + jnp.einsum(
            "mnk,mp->nkp", rounded[:, :, 1], table_rows[1], preferred_element_type=jnp.float32
        )
        scores = scores * scale
        return jnp.max(scores.reshape(block_rows_each, shifts, class_count, angles), axis=(1, 3))

    block_indices = jnp.arange(group_rows // block_rows_each, dtype=jnp.int32)
    best_scores = lax.map(score_block, block_indices).reshape(group_rows, class_count)
    local_ids = all_ids - cls_index * class_count
    valid_mask = jnp.arange(list_length, dtype=jnp.int32)[None, :] < all_counts[:, None]
    kept = jnp.where(valid_mask, all_weights, jnp.zeros_like(all_weights))
    class_hit = local_ids[:, :, None] == jnp.arange(class_count, dtype=jnp.int32)[None, None, :]
    selection = jnp.where(class_hit, kept[:, :, None], jnp.zeros((), jnp.bfloat16))
    shift_hit = (
        all_shifts[:, :, None] == jnp.arange(shifts, dtype=jnp.int32)[None, None, :]
    ).astype(jnp.bfloat16)
    chosen = jnp.einsum("ijs,misc->mijc", shift_hit, all_images, preferred_element_type=jnp.float32)
    slot_images = chosen.astype(jnp.bfloat16).reshape(angles, group_rows * list_length, cycle_parts)
    slot_weights = jnp.broadcast_to(
        selection.reshape(1, group_rows * list_length, class_count),
        (dom_size, group_rows * list_length, class_count),
    )
    received_images, received_weights = (
        lax.all_to_all(slot_images, "dom", split_axis=0, concat_axis=1, tiled=True),
        lax.all_to_all(slot_weights, "dom", split_axis=0, concat_axis=1, tiled=True),
    )
    weight_rows = received_weights[0]
    class_sums = jnp.einsum(
        "nk,mnc->mkc", weight_rows, received_images, preferred_element_type=jnp.float32
    )
    totals = jnp.sum(weight_rows.astype(jnp.float32), axis=0)
    class_means = class_sums / jnp.maximum(totals, 1.0)[None, :, None]
    return (best_scores, class_means)


def solution(mesh):
    return jax.shard_map(
        on_device,
        mesh=mesh,
        in_specs=(
            P(None, ("dom", "cls"), None, None),
            P(None, "cls", None),
            P(("dom", "cls"), None),
            P(("dom", "cls")),
            P(("dom", "cls"), None),
            P(("dom", "cls"), None),
        ),
        out_specs=(P("dom", "cls"), P("dom", "cls", None)),
        check_vma=False,
    )
```

profile of v0, /device:TPU:17, one launch (start us, length us, event | category | flops | bytes accessed | tf_op | source)
XLA Modules:
  0.0 179.0 jit_solution(16337592489161478630)
XLA Ops:
  7.3 3.8 %copy.41 = bf16[256,4,9,128]{3,0,2,1:T(8,128)(2,1)} copy(bf16[256,4,9,128]{3,1,2,0:T(4,128)(2,1)} %param.8) | data formatting | bytes 4718592 | tf_op args[0]
  11.1 5.6 %all-gather.2 = bf16[4,4,3]{2,1,0:T(4,128)(2,1)S(1)} all-gather(bf16[1,4,3]{2,1,0:T(4,128)(2,1)S(1)} %bitcast.81), channel_id=1, replica_groups=mesh['dom'=8,'cls'=4] {'cls'}, dimensions={0}, use_global_device_ids=true | all-gather | bytes 120 | tf_op jit(solution)/shard_map/all_gather | solution.py:37
  16.6 5.1 %all-gather.1 = s32[4,4,3]{2,1,0:T(4,128)S(1)} all-gather(s32[1,4,3]{2,1,0:T(4,128)S(1)} %bitcast.79), channel_id=1, replica_groups=mesh['dom'=8,'cls'=4] {'cls'}, dimensions={0}, use_global_device_ids=true | all-gather | bytes 240 | tf_op jit(solution)/shard_map/all_gather | solution.py:34
  23.5 4.5 %all-reduce = s32[16]{0:T(128)S(1)} all-reduce(s32[16]{0:T(128)S(1)} %dynamic-update-slice), channel_id=1, replica_groups=mesh['dom'=8,'cls'=4] {'cls'}, use_global_device_ids=true, to_apply=%add | all-reduce | flops 16 | bytes 128
  29.1 5.6 %all-to-all-start.1 = ((bf16[8,2,1200]{2,1,0:T(2,128)(2,1)}), bf16[8,2,1200]{2,1,0:T(2,128)(2,1)S(1)}, u32[]{:S(2)}, u32[]{:S(2)}) async-start(bf16[8,2,1200]{2,1,0:T(2,128)(2,1)} %reshape.144), calls=%async_computation.1 | async-start | bytes 81920 | tf_op jit(solution)/shard_map/all_to_all | solution.py:83
  34.7 2.2 %copy.44 = bf16[256,50,128]{2,1,0:T(8,128)(2,1)S(1)} copy(bf16[256,50,128]{2,0,1:T(8,128)(2,1)S(1)} %copy-done) | data formatting | bytes 6553600 | tf_op args[1]
  36.9 6.2 %all-gather = s32[4,4,3]{2,1,0:T(4,128)S(1)} all-gather(s32[1,4,3]{2,1,0:T(4,128)S(1)} %bitcast.80), channel_id=1, replica_groups=mesh['dom'=8,'cls'=4] {'cls'}, dimensions={0}, use_global_device_ids=true | all-gather | bytes 240 | tf_op jit(solution)/shard_map/all_gather | solution.py:36
  43.1 1.1 negate_convert_fusion
  44.2 1.5 slice_negate_fusion
  45.7 6.5 %maximum_maximum_fusion = bf16[256,100,128]{2,1,0:T(8,128)(2,1)} fusion(bf16[256,50,64]{2,1,0:T(8,128)(2,1)S(1)} %get-tuple-element.68, bf16[256,50,64]{2,1,0:T(8,128)(2,1)S(1)} %get-tuple-element.67, bf16[256,50,128]{2,1,0:T(8,128)(2,1)S(1)} %copy.44), kind=kLoop, calls=%fused_computation.15 | loop fusion | flops 19660800 | bytes 13107200 | tf_op jit(solution)/shard_map/concatenate | solution.py:20
  52.5 24.6 %all-gather.5.cloned.1.call-done = bf16[256,16,9,128]{3,0,2,1:T(8,128)(2,1)} async-done(((bf16[256,4,9,128]{3,0,2,1:T(8,128)(2,1)}), bf16[256,16,9,128]{3,0,2,1:T(8,128)(2,1)}) %all-gather.5.cloned.1.call-update) | async-done | bytes 9437200 | tf_op jit(solution)/shard_map/all_gather | solution.py:33
  77.1 9.7 %fusion.15 = bf16[256,16,3,128]{3,2,0,1:T(4,128)(2,1)S(1)} fusion(bf16[256,16,9,128]{3,0,2,1:T(8,128)(2,1)} %all-gather.5.cloned.1.call-done, s32[16,3]{1,0:T(8,128)S(1)} %bitcast.75), kind=kOutput, calls=%fused_computation.17 | convolution fusion | flops 29884848 | bytes 12583104 | tf_op jit(solution)/shard_map/ijs,misc->mijc/dot_general | solution.py:75
  87.7 3.7 %copy.49 = bf16[256,48,128]{2,1,0:T(8,128)(2,1)} copy(bf16[256,48,128]{2,0,1:T(8,128)(2,1)S(1)} %bitcast.74) | data formatting | bytes 6291456 | tf_op jit(solution)/shard_map/reshape | solution.py:76
  91.4 5.5 %all-to-all-start = ((bf16[256,48,128]{2,1,0:T(8,128)(2,1)}), bf16[256,48,128]{2,1,0:T(8,128)(2,1)}, u32[]{:S(2)}, u32[]{:S(2)}) async-start(bf16[256,48,128]{2,1,0:T(8,128)(2,1)} %copy.49), calls=%async_computation | async-start | bytes 6291456 | tf_op jit(solution)/shard_map/all_to_all | solution.py:82
  96.9 71.6 %while.10 = (s32[]{:T(128)}, f32[4,4,50]{2,1,0:T(4,128)S(1)}, s32[4]{0:T(128)S(1)}, bf16[256,16,9,128]{3,0,2,1:T(8,128)(2,1)}, bf16[256,100,128]{2,1,0:T(8,128)(...) while((s32[]{:T(128)}, f32[4,4,50]{2,1,0:T(4,128)S(1)}, ...), condition=%wide.region_3.4_spmd, body=%wide.region_0.3_spmd.sunk | while | flops 710092608 | bytes 29099092 | solution.py:66
  98.1 1.8 %constant_dynamic-slice_fusion.2 = bf16[256,4,9,128]{3,0,2,1:T(8,128)(2,1)S(1)} fusion(bf16[256,16,9,128]{3,0,2,1:T(8,128)(2,1)} %get-tuple-element.137, s32[]{:T(128)S(6)} %select_n.50), kind=kLoop, calls=%fused_computation.12.clone.1 | loop fusion | bytes 4718596 | tf_op jit(solution)/shard_map/while/body/eval_jaxpr/dynamic_slice | solution.py:46
  100.0 8.2 %fusion.46 = bf16[256,36,100]{2,1,0:T(8,128)(2,1)S(1)} fusion(bf16[256,100,128]{2,1,0:T(8,128)(2,1)} %get-tuple-element.138, bf16[256,36,128]{2,0,1:T(8,128)(2,1)S(1)} %bitcast.72), kind=kOutput, calls=%fused_computation.2.clone.1 | convolution fusion | flops 236851200 | bytes 10756096 | tf_op jit(solution)/shard_map/while/body/eval_jaxpr/mnc,mqc->mnq/dot_general | solution.py:50
  108.2 3.9 %copy.80 = bf16[256,36,100]{0,1,2:T(8,128)(2,1)} copy(bf16[256,36,100]{2,1,0:T(8,128)(2,1)S(1)} %fusion.46) | data formatting | bytes 3686400 | tf_op jit(solution)/shard_map/while/body/eval_jaxpr/convert_element_type | solution.py:53
  112.1 1.7 fusion.47
  116.1 1.8 %constant_dynamic-slice_fusion.2 = bf16[256,4,9,128]{3,0,2,1:T(8,128)(2,1)S(1)} fusion(bf16[256,16,9,128]{3,0,2,1:T(8,128)(2,1)} %get-tuple-element.137, s32[]{:T(128)S(6)} %select_n.50), kind=kLoop, calls=%fused_computation.12.clone.1 | loop fusion | bytes 4718596 | tf_op jit(solution)/shard_map/while/body/eval_jaxpr/dynamic_slice | solution.py:46
  117.9 8.2 %fusion.46 = bf16[256,36,100]{2,1,0:T(8,128)(2,1)S(1)} fusion(bf16[256,100,128]{2,1,0:T(8,128)(2,1)} %get-tuple-element.138, bf16[256,36,128]{2,0,1:T(8,128)(2,1)S(1)} %bitcast.72), kind=kOutput, calls=%fused_computation.2.clone.1 | convolution fusion | flops 236851200 | bytes 10756096 | tf_op jit(solution)/shard_map/while/body/eval_jaxpr/mnc,mqc->mnq/dot_general | solution.py:50
  126.1 3.9 %copy.80 = bf16[256,36,100]{0,1,2:T(8,128)(2,1)} copy(bf16[256,36,100]{2,1,0:T(8,128)(2,1)S(1)} %fusion.46) | data formatting | bytes 3686400 | tf_op jit(solution)/shard_map/while/body/eval_jaxpr/convert_element_type | solution.py:53
  130.0 1.7 fusion.47
  134.0 1.8 %constant_dynamic-slice_fusion.2 = bf16[256,4,9,128]{3,0,2,1:T(8,128)(2,1)S(1)} fusion(bf16[256,16,9,128]{3,0,2,1:T(8,128)(2,1)} %get-tuple-element.137, s32[]{:T(128)S(6)} %select_n.50), kind=kLoop, calls=%fused_computation.12.clone.1 | loop fusion | bytes 4718596 | tf_op jit(solution)/shard_map/while/body/eval_jaxpr/dynamic_slice | solution.py:46
  135.8 8.2 %fusion.46 = bf16[256,36,100]{2,1,0:T(8,128)(2,1)S(1)} fusion(bf16[256,100,128]{2,1,0:T(8,128)(2,1)} %get-tuple-element.138, bf16[256,36,128]{2,0,1:T(8,128)(2,1)S(1)} %bitcast.72), kind=kOutput, calls=%fused_computation.2.clone.1 | convolution fusion | flops 236851200 | bytes 10756096 | tf_op jit(solution)/shard_map/while/body/eval_jaxpr/mnc,mqc->mnq/dot_general | solution.py:50
  144.0 3.9 %copy.80 = bf16[256,36,100]{0,1,2:T(8,128)(2,1)} copy(bf16[256,36,100]{2,1,0:T(8,128)(2,1)S(1)} %fusion.46) | data formatting | bytes 3686400 | tf_op jit(solution)/shard_map/while/body/eval_jaxpr/convert_element_type | solution.py:53
  147.9 1.7 fusion.47
  151.9 1.8 %constant_dynamic-slice_fusion.2 = bf16[256,4,9,128]{3,0,2,1:T(8,128)(2,1)S(1)} fusion(bf16[256,16,9,128]{3,0,2,1:T(8,128)(2,1)} %get-tuple-element.137, s32[]{:T(128)S(6)} %select_n.50), kind=kLoop, calls=%fused_computation.12.clone.1 | loop fusion | bytes 4718596 | tf_op jit(solution)/shard_map/while/body/eval_jaxpr/dynamic_slice | solution.py:46
  153.7 8.2 %fusion.46 = bf16[256,36,100]{2,1,0:T(8,128)(2,1)S(1)} fusion(bf16[256,100,128]{2,1,0:T(8,128)(2,1)} %get-tuple-element.138, bf16[256,36,128]{2,0,1:T(8,128)(2,1)S(1)} %bitcast.72), kind=kOutput, calls=%fused_computation.2.clone.1 | convolution fusion | flops 236851200 | bytes 10756096 | tf_op jit(solution)/shard_map/while/body/eval_jaxpr/mnc,mqc->mnq/dot_general | solution.py:50
  161.9 3.9 %copy.80 = bf16[256,36,100]{0,1,2:T(8,128)(2,1)} copy(bf16[256,36,100]{2,1,0:T(8,128)(2,1)S(1)} %fusion.46) | data formatting | bytes 3686400 | tf_op jit(solution)/shard_map/while/body/eval_jaxpr/convert_element_type | solution.py:53
  165.8 1.7 fusion.47
  168.6 2.6 %fusion.19 = f32[32,50,128]{2,1,0:T(8,128)S(1)} fusion(bf16[32,8,48,128]{3,2,0,1:T(8,128)(2,1)} %bitcast.18, f32[50]{0:T(128)S(1)} %broadcast_maximum_fusion, bf16[8,48,50]{2,1,0:T(8,128)(2,1)S(1)} %reshape.145), kind=kOutput, calls=%fused_computation.21 | convolution fusion | flops 157491200 | bytes 4003528 | tf_op jit(solution)/shard_map/nk,mnc->mkc/dot_general | solution.py:86
  (62 shorter events, 11.0 us)
Async XLA Ops:
  7.2 14.8 %copy-start.6 = (u32[32]{0:T(128)S(1)}, u32[32]{0:T(128)}, u32[]{:S(2)}) copy-start(u32[32]{0:T(128)} %constant.57) | copy-start | bytes 388
  7.2 3.9 %copy-start.3 = (bf16[4,3]{1,0:T(4,128)(2,1)S(1)}, bf16[4,3]{1,0:T(4,128)(2,1)}, u32[]{:S(2)}) copy-start(bf16[4,3]{1,0:T(4,128)(2,1)} %param.13) | copy-start | bytes 76
  7.2 9.5 %copy-start.1 = (s32[4,3]{1,0:T(4,128)S(1)}, s32[4,3]{1,0:T(4,128)}, u32[]{:S(2)}) copy-start(s32[4,3]{1,0:T(4,128)} %param.10) | copy-start | bytes 148
  7.2 16.0 %copy-start.5 = (s32[4]{0:T(128)S(1)}, s32[4]{0:T(128)}, u32[]{:S(2)}) copy-start(s32[4]{0:T(128)} %param.11) | copy-start | bytes 52
  7.2 27.5 %copy-start = (bf16[256,50,128]{2,0,1:T(8,128)(2,1)S(1)}, bf16[256,50,128]{2,0,1:T(8,128)(2,1)}, u32[]{:S(2)}) copy-start(bf16[256,50,128]{2,0,1:T(8,128)(2,1)} %param.9) | copy-start | bytes 9830404
  7.2 69.9 %all-gather.5.cloned.1.call-start = ((), (), s32[]{:S(2)}) async-start(), calls=%async_computation.2 | async-start | bytes 11796480 | tf_op jit(solution)/shard_map/all_gather | solution.py:33
  21.8 15.1 %copy-start.2 = (s32[4,3]{1,0:T(4,128)S(1)}, s32[4,3]{1,0:T(4,128)}, u32[]{:S(2)}) copy-start(s32[4,3]{1,0:T(4,128)} %param.12) | copy-start | bytes 148
  29.1 23.1 %all-to-all-start.1 = ((bf16[8,2,1200]{2,1,0:T(2,128)(2,1)}), bf16[8,2,1200]{2,1,0:T(2,128)(2,1)S(1)}, u32[]{:S(2)}, u32[]{:S(2)}) async-start(bf16[8,2,1200]{2,1,0:T(2,128)(2,1)} %reshape.144), calls=%async_computation.1 | async-start | bytes 81920 | tf_op jit(solution)/shard_map/all_to_all | solution.py:83
  91.4 77.1 %all-to-all-start = ((bf16[256,48,128]{2,1,0:T(8,128)(2,1)}), bf16[256,48,128]{2,1,0:T(8,128)(2,1)}, u32[]{:S(2)}, u32[]{:S(2)}) async-start(bf16[256,48,128]{2,1,0:T(8,128)(2,1)} %copy.49), calls=%async_computation | async-start | bytes 6291456 | tf_op jit(solution)/shard_map/all_to_all | solution.py:82
  168.5 3.6 %copy-start.4 = (f32[4,4,50]{2,1,0:T(4,128)}, f32[4,4,50]{2,1,0:T(4,128)S(1)}, u32[]{:S(2)}) copy-start(f32[4,4,50]{2,1,0:T(4,128)S(1)} %get-tuple-element.34) | copy-start | bytes 9604
Sparse Core Ops, SparseCore 0:
  11.2 65.8 all-gather.4
where the time goes:
time: 181 us; the launch traced here: 179 us
  matrix products  49.2 us (27%)
  local copies, waits for them, and re-layouts  45.6 us (25%)
  waiting for transfers between devices  24.6 us (14%)
  blocking collectives  21.4 us (12%)
  between operations  14.9 us (8%)
  starting transfers between devices  11.1 us (6%)
  other arithmetic  9.39 us (5%)
  loops' own time  2.78 us (2%)
    dot_general x4, matrix products, score_block(): jnp.einsum('mnc,mqc->mnq', flat_block, stacked, preferred_element_type=jn...  32.8 us
    all_gather x1, waiting for transfers between devices, on_device(): lax.all_gather(particles, 'cls', axis=1, tiled=True)  24.6 us
    convert_element_type x4, local copies, waits for them, and re-layouts, score_block(): products.astype(jnp.bfloat16)  15.5 us
    dot_general x1, matrix products, on_device(): jnp.einsum('ijs,misc->mijc', shift_hit, all_images, preferred_element_typ...  9.7 us
    unnamed x23, local copies, waits for them, and re-layouts  8.89 us
    dynamic_slice x4, local copies, waits for them, and re-layouts, score_block(): lax.dynamic_slice_in_dim(all_images, block_index * block_rows_each, block...  7.29 us
    slice x4, local copies, waits for them, and re-layouts, score_block(): rounded[:, :, 1]  6.63 us
    concatenate x1, other arithmetic, real_form(): return jnp.concatenate([references, swapped], axis=1)  6.49 us
  transfers between devices with their start and end apart: 3, of which 1 were waited for; matrix products, arithmetic and copies ran while one was open for 46% of the time, Pallas kernels for 0%

commit v1 on v0

v1 whole, which is shorter than its diff:
```python
import functools
import math

import jax
import jax.numpy as jnp
from jax import lax
from jax.experimental import pallas as pl
from jax.experimental.pallas import tpu as pltpu
from jax.sharding import PartitionSpec as P

VMEM_LIMIT = 56 * 1024 * 1024


def up(value, unit):
    return -(-value // unit) * unit


def half_table(angles):
    rows = angles // 2 + 1
    padded = up(rows, 8)
    rotation = jnp.arange(padded, dtype=jnp.int32)
    rotation = jnp.where(rotation < rows, rotation, 0)
    product = rotation[:, None] * jnp.arange(angles, dtype=jnp.int32)[None, :] % angles
    phase_angle = product.astype(jnp.float32) * (2.0 * math.pi / angles)
    return jnp.concatenate([jnp.cos(phase_angle), -jnp.sin(phase_angle)]).astype(jnp.bfloat16)


def score_kernel(dims, x_ref, w_ref, t_ref, out_ref, held):
    groups, each, shifts, angles, chunk, slots, kpad, scale = dims
    rows = each * shifts
    step = pl.program_id(1)
    first = step * chunk

    def quad(index, carry):
        blocks = [
            x_ref[c, pl.ds(pl.multiple_of(index * 4 * rows, 16), 4 * rows), :] for c in range(groups)
        ]
        for part in range(4):
            start = part * rows // 16 * 16
            offset = part * rows - start
            size = up(offset + rows, 16)
            skip = offset // 8 * 8
            lhs = jnp.concatenate([b[start : start + size] for b in blocks], axis=0)
            prod = lax.dot_general(
                lhs, w_ref[index * 4 + part], (((1,), (1,)), ((), ())), preferred_element_type=jnp.float32
            )
            keep = up(offset - skip + rows, 8)
            slot = 8 - (offset - skip)
            for c in range(groups):
                value = prod[c * size + skip : c * size + skip + keep]
                begin = (c * slots + slot) * angles + first + index * 4 + part
                held[pl.ds(begin, keep, stride=angles), :] = value
        return carry

    lax.fori_loop(0, chunk // 4, quad, 0, unroll=2)

    @pl.when(step == pl.num_programs(1) - 1)
    def _():
        table = t_ref[...]
        half = table.shape[0] // 2
        width = 2 * kpad

        for c in range(groups):

            def one_shift(s, best):
                best = list(best)
                for pair in range(0, each, 2):
                    cols = []
                    for i in (pair, pair + 1):
                        at = pl.multiple_of((c * slots + 8 + s * each + i) * angles, angles)
                        cols.append(held[pl.ds(at, angles), :].astype(jnp.bfloat16))
                    both = jnp.dot(table, jnp.concatenate(cols, axis=1), preferred_element_type=jnp.float32)
                    for h in range(2):
                        even = both[:half, h * width : (h + 1) * width]
                        odd = pltpu.roll(both[half:, h * width : (h + 1) * width], kpad, 1)
                        total = even + jnp.abs(odd)
                        top = jnp.max(total.reshape(half // 8, 8, width), axis=0)
                        best[pair + h] = jnp.maximum(best[pair + h], top)
                return tuple(best)

            start = tuple(jnp.full((8, width), -jnp.inf, jnp.float32) for _ in range(each))
            best = lax.fori_loop(0, shifts, one_shift, start)
            for i in range(each):
                out_ref[c * each + i : c * each + i + 1, :] = jnp.max(best[i], axis=0, keepdims=True) * scale


def score(images, weights_of, table, each, shifts):
    all_groups = images.shape[0]
    groups = math.gcd(all_groups, 4)
    angles, width, parts = weights_of.shape
    rows = each * shifts
    chunk = 32
    slots = up(rows + 16, 4)
    scale = 1.0 / math.sqrt(float(parts * angles))
    dims = (groups, each, shifts, angles, chunk, slots, width // 2, scale)
    return pl.pallas_call(
        functools.partial(score_kernel, dims),
        out_shape=jax.ShapeDtypeStruct((all_groups * each, width), jnp.float32),
        grid=(all_groups // groups, angles // chunk),
        in_specs=[
            pl.BlockSpec((groups, chunk * rows, parts), lambda b, g: (b, g, 0)),
            pl.BlockSpec((chunk, width, parts), lambda b, g: (g, 0, 0)),
            pl.BlockSpec(table.shape, lambda b, g: (0, 0)),
        ],
        out_specs=pl.BlockSpec((groups * each, width), lambda b, g: (b, 0)),
        scratch_shapes=[pltpu.VMEM((groups * slots * angles, width), jnp.float32)],
        compiler_params=pltpu.CompilerParams(vmem_limit_bytes=VMEM_LIMIT),
        name="score",
    )(images, weights_of, table)


def mean_kernel(block, own, x_ref, s_ref, d_ref, out_ref):
    many = x_ref.shape[0]
    parts = x_ref.shape[2]
    classes = d_ref.shape[0]
    weights = s_ref[...]
    scale = d_ref[...]

    def body(index, carry):
        rows = x_ref[:, pl.ds(pl.multiple_of(index * block, 16), block), :].reshape(many * block, parts)
        sums = jnp.dot(weights, rows, preferred_element_type=jnp.float32)
        for part in range(4):
            value = sums[part * classes : (part + 1) * classes] / scale
            out_ref[pl.ds(index * 4 + part, classes, stride=own), :] = value
        return carry

    lax.fori_loop(0, own // 4, body, 0)


def on_device(particles, references, class_ids, counts, shift_ids, weights):
    dom_size = lax.axis_size("dom")
    cls_size = lax.axis_size("cls")
    cls_index = lax.axis_index("cls")
    angles, class_count, parts = references.shape
    cycles = parts // 2
    each, shifts = particles.shape[1:3]
    length = class_ids.shape[1]
    own = angles // dom_size

    ordered = jnp.transpose(particles, (0, 2, 1, 3))
    images = lax.all_gather(ordered.reshape(angles * shifts * each, parts), "cls", axis=0)

    valid = jnp.arange(length, dtype=jnp.int32)[None, :] < counts[:, None]
    kept = jnp.where(valid, weights.astype(jnp.float32), 0.0)
    packed = jnp.stack([class_ids.astype(jnp.float32).T, kept.T])
    listing = lax.all_gather(packed, ("dom", "cls"), axis=0)

    shift_of = shift_ids.T[None, :, :, None]
    chosen = jnp.broadcast_to(ordered[:, 0:1], (angles, length, each, parts))
    for s in range(1, shifts):
        chosen = jnp.where(shift_of == s, ordered[:, s : s + 1], chosen)
    sent = chosen.reshape(dom_size, own * length * each, parts)
    received = lax.all_to_all(sent, "dom", split_axis=0, concat_axis=0, tiled=True)
    received = lax.all_gather(received, "cls", axis=0)
    received = received.reshape(cls_size * dom_size, own * length * each, parts)

    kpad = up(class_count, 64)
    swapped = jnp.concatenate([-references[:, :, cycles:], references[:, :, :cycles]], axis=2)
    margin = ((0, 0), (0, kpad - class_count), (0, 0))
    stacked = jnp.concatenate([jnp.pad(references, margin), jnp.pad(swapped, margin)], axis=1)
    best = score(images, stacked, half_table(angles), each, shifts)[:, :class_count]

    listing = listing.reshape(dom_size, cls_size, 2, length * each).transpose(2, 1, 0, 3)
    local = listing[0].reshape(-1, length * each) - (cls_index * class_count).astype(jnp.float32)
    kept_all = listing[1].reshape(-1, length * each)
    mine = local[None] == jnp.arange(class_count, dtype=jnp.int32).astype(jnp.float32)[:, None, None]
    picked = jnp.where(mine, kept_all[None], 0.0)
    totals = jnp.maximum(jnp.sum(picked, axis=(1, 2)), 1.0)
    kept_rows = up(class_count, 8)
    picked = jnp.pad(picked, ((0, kept_rows - class_count), (0, 0), (0, 0))).astype(jnp.bfloat16)
    totals = jnp.pad(totals, (0, kept_rows - class_count), constant_values=1.0)
    many = cls_size * dom_size
    spread = jnp.eye(4, dtype=jnp.bfloat16)[:, None, None, :, None] * picked[None, :, :, None, :]
    block = 4 * length * each
    spread = spread.reshape(4 * kept_rows, many * block)
    means = pl.pallas_call(
        functools.partial(mean_kernel, block, own),
        out_shape=jax.ShapeDtypeStruct((kept_rows * own, parts), jnp.float32),
        in_specs=[pl.BlockSpec(memory_space=pltpu.VMEM)] * 3,
        out_specs=pl.BlockSpec(memory_space=pltpu.VMEM),
        compiler_params=pltpu.CompilerParams(vmem_limit_bytes=VMEM_LIMIT),
        name="means",
    )(received, spread, jnp.broadcast_to(totals[:, None], (kept_rows, parts)))
    means = means.reshape(kept_rows, own, parts)[:class_count]
    return (best, jnp.transpose(means, (1, 0, 2)))


def solution(mesh):
    return jax.shard_map(
        on_device,
        mesh=mesh,
        in_specs=(
            P(None, ("dom", "cls"), None, None),
            P(None, "cls", None),
            P(("dom", "cls"), None),
            P(("dom", "cls")),
            P(("dom", "cls"), None),
            P(("dom", "cls"), None),
        ),
        out_specs=(P("dom", "cls"), P("dom", "cls", None)),
        check_vma=False,
    )
```

time: 181 us -> 184 us (1.017)
  matrix products: 49.2 us -> 0 us
  Pallas kernels: 0 us -> 41.9 us
  blocking collectives: 21.4 us -> 57.2 us
  local copies, waits for them, and re-layouts: 45.6 us -> 17.8 us
  waiting for transfers between devices: 24.6 us -> 36.9 us
  starting transfers between devices: 11.1 us -> 0.08 us
  other arithmetic: 9.39 us -> 14.3 us
  loops' own time: 2.78 us -> 0 us
    dot_general x14 -> x0, matrix products: 49.2 us -> none  [the longest x4 32.8 us: score_block(): jnp.einsum('mnc,mqc->mnq', flat_block, stacked, preferred_element_type=jn...]
    pallas_call x0 -> x2, Pallas kernels: none -> 41.9 us  [the longest x1 35.6 us: score(): pl.pallas_call(functools.partial(score_kernel, dims), out_shape=jax.Shape...]
    all_to_all x0 -> x1, blocking collectives: none -> 23.6 us  [on_device(): lax.all_to_all(sent, 'dom', split_axis=0, concat_axis=0, tiled=True)]
    all_gather x3 -> x1, blocking collectives: 16.9 us -> 33.6 us  [on_device(): listing = lax.all_gather(packed, ('dom', 'cls'), axis=0)]
    convert_element_type x5 -> x0, local copies, waits for them, and re-layouts: 16.4 us -> none  [the longest x4 15.5 us: score_block(): products.astype(jnp.bfloat16)]
    all_gather x1 -> x2, waiting for transfers between devices: 24.6 us -> 36.2 us  [the longest x1 36.2 us: on_device(): lax.all_gather(ordered.reshape(angles * shifts * each, parts), 'cls', axi...]
    all_to_all x2 -> x0, starting transfers between devices: 11 us -> none  [the longest x1 5.58 us: on_device(): lax.all_to_all(slot_weights, 'dom', split_axis=0, concat_axis=1, tiled=True)]
    dynamic_slice x8 -> x0, local copies, waits for them, and re-layouts: 9.63 us -> none  [the longest x4 7.29 us: score_block(): lax.dynamic_slice_in_dim(all_images, block_index * block_rows_each, block...]
  transfers between devices with their start and end apart: 3 -> 2, of which waited for: 1 -> 1; matrix products, arithmetic and copies ran while one was open for 46% -> 11% of each run, Pallas kernels for 0% -> 3%
where the time goes in v1:
time: 184 us; the launch traced here: 183 us
  blocking collectives  57.2 us (31%)
  Pallas kernels  41.9 us (23%)
  waiting for transfers between devices  36.9 us (20%)
  local copies, waits for them, and re-layouts  17.8 us (10%)
  between operations  14.4 us (8%)
  other arithmetic  14.3 us (8%)
    all_gather x1, waiting for transfers between devices, on_device(): lax.all_gather(ordered.reshape(angles * shifts * each, parts), 'cls', axi...  36.2 us
    pallas_call x1, Pallas kernels, score(): pl.pallas_call(functools.partial(score_kernel, dims), out_shape=jax.Shape...  35.6 us
    all_gather x1, blocking collectives, on_device(): listing = lax.all_gather(packed, ('dom', 'cls'), axis=0)  33.6 us
    all_to_all x1, blocking collectives, on_device(): lax.all_to_all(sent, 'dom', split_axis=0, concat_axis=0, tiled=True)  23.6 us
    pallas_call x1, Pallas kernels, on_device(): pl.pallas_call(functools.partial(mean_kernel, block, own), out_shape=jax....  6.33 us
    unnamed x9, local copies, waits for them, and re-layouts  4.54 us
    broadcast_in_dim x24, local copies, waits for them, and re-layouts, on_device(): chosen = jnp.where(shift_of == s, ordered[:, s:s + 1], chosen)  4.42 us
    select_n x1, other arithmetic, on_device(): chosen = jnp.where(shift_of == s, ordered[:, s:s + 1], chosen)  3.98 us
  transfers between devices with their start and end apart: 2, of which 1 were waited for; matrix products, arithmetic and copies ran while one was open for 11% of the time, Pallas kernels for 3%

profile of v1, /device:TPU:17, one launch (start us, length us, event | category | flops | bytes accessed | tf_op | source)
XLA Modules:
  0.0 182.6 jit_solution(15969533684435633363)
XLA Ops:
  7.2 2.7 %slice_bitcast_fusion = (bf16[256,4,128]{2,1,0:T(4,128)(2,1)S(1)}, bf16[256,4,128]{2,1,0:T(4,128)(2,1)S(1)}, bf16[256,4,128]{2,1,0:T(4,128)(2,1)S(1)}, bf16[256,...) fusion(bf16[256,9,4,128]{3,2,1,0:T(4,128)(2,1)} %bitcast.65), kind=kLoop, calls=%fused_computation.12 | loop fusion | bytes 4718592 | tf_op jit(solution)/shard_map/broadcast_in_dim | solution.py:149
  10.1 0.3 broadcast_in_dim.198
  10.6 0.3 broadcast_in_dim.204
  11.0 0.3 broadcast_in_dim.210
  11.5 0.3 broadcast_in_dim.216
  11.9 0.3 broadcast_in_dim.222
  12.4 0.3 broadcast_in_dim.228
  12.9 0.3 broadcast_in_dim.234
  13.3 0.3 broadcast_in_dim.240
  13.8 0.2 broadcast_in_dim.219
  14.3 0.2 broadcast_in_dim.231
  14.5 0.2 broadcast_in_dim.237
  14.7 0.2 broadcast_in_dim.243
  15.5 4.0 %select_select_fusion = bf16[8,384,128]{2,1,0:T(8,128)(2,1)S(1)} fusion(bf16[8,384,128]{2,1,0:T(8,128)(2,1)S(1)} %bitcast.74, bf16[8,384,128]{2,1,0:T(8,128)(2,1)S(1)} %bitcast.75, bf16[8,384,128]{2,1,0:T(8,128)(2,1)S(1)} %bitcast.67, bf16[8,384,128]{2,1,0:T(8,128)(2,1)S(1)} %bitcast.68, bf16[8,384,128]{2,1,0:T(8,128)(2,1)S(1)} %bitcast.69, ...), kind=kLoop, calls=%fused_computation.9 | loop fusion | flops 3145728 | bytes 7888896 | tf_op jit(solution)/shard_map/jit(_where)/select_n | solution.py:151
  19.6 23.6 %all_to_all.5 = bf16[8,384,128]{2,1,0:T(8,128)(2,1)} all-to-all(bf16[8,384,128]{2,1,0:T(8,128)(2,1)S(1)} %select_select_fusion), channel_id=1, replica_groups=mesh['dom'=8,'cls'=4] {'dom'}, dimensions={0} | all-to-all | bytes 1572864 | tf_op jit(solution)/shard_map/all_to_all | solution.py:153
  43.3 0.7 all-gather.5.cloned.1.call-update
  44.3 33.6 %all-gather.1 = f32[64,3,4]{2,1,0:T(4,128)S(1)} all-gather(f32[2,3,4]{2,1,0:T(4,128)S(1)} %pad_maximum_fusion.1), channel_id=3, replica_groups=mesh['dom'=8,'cls'=4] {'dom','cls'}, dimensions={0}, use_global_device_ids=true | all-gather | bytes 3168 | tf_op jit(solution)/shard_map/all_gather | solution.py:146
  78.3 0.7 broadcast_multiply_fusion
  79.0 0.9 mul.56
  79.8 1.1 copy.67.s_ref
  81.0 4.5 %copy.53 = bf16[256,50,128]{2,1,0:T(8,128)(2,1)S(1)} copy(bf16[256,50,128]{2,0,1:T(8,128)(2,1)} %param.7) | data formatting | bytes 6553600 | tf_op args[1]
  85.5 0.2 select_reduce_fusion
  85.7 0.6 cosine_convert_fusion
  86.4 0.7 pad_maximum_fusion.t_ref
  87.0 1.5 slice_negate_fusion
  88.6 2.3 %fusion.4 = bf16[256,64,128]{2,1,0:T(8,128)(2,1)S(1)} fusion(bf16[256,50,64]{2,1,0:T(8,128)(2,1)S(1)} %get-tuple-element.3, bf16[256,50,64]{2,1,0:T(8,128)(2,1)S(1)} %get-tuple-element.2), kind=kLoop, calls=%fused_computation.6 | loop fusion | flops 14680064 | bytes 7471104 | tf_op jit(solution)/shard_map/concatenate | solution.py:158
  90.9 4.0 %fusion.1.w_ref = bf16[256,128,128]{2,1,0:T(8,128)(2,1)} fusion(bf16[256,50,128]{2,1,0:T(8,128)(2,1)S(1)} %copy.53, bf16[256,64,128]{2,1,0:T(8,128)(2,1)S(1)} %fusion.4), kind=kLoop, calls=%fused_computation.2 | loop fusion | flops 25165824 | bytes 15859712 | tf_op jit(solution)/shard_map/concatenate | solution.py:160
  94.9 0.7 broadcast_in_dim.252.d_ref
  95.5 6.3 %means.1 = f32[1792,128]{1,0:T(8,128)} custom-call(bf16[32,384,128]{2,1,0:T(8,128)(2,1)} %all-gather.7.cloned.1.call-done.x_ref, bf16[224,1536]{1,0:T(8,128)(2,1)} %copy.67.s_ref, f32[56,128]{1,0:T(8,128)} %broadcast_in_dim.252.d_ref), custom_call_target="tpu_custom_call" | custom-call | tf_op jit(solution)/shard_map/means/pallas_call | solution.py:176
  101.9 2.1 %slice.78 = f32[1600,128]{1,0:T(8,128)} slice(f32[1792,128]{1,0:T(8,128)} %means.1), slice={[0:1600], [0:128]} | slice | bytes 1638400 | tf_op jit(solution)/shard_map/slice | solution.py:184
  104.0 36.2 %all-gather.5.cloned.1.call-done.x_ref = bf16[4,9216,128]{2,1,0:T(8,128)(2,1)} async-done(((bf16[1,9216,128]{2,1,0:T(8,128)(2,1)}), bf16[4,9216,128]{2,1,0:T(8,128)(2,1)}) %all-gather.5.cloned.1.call-update) | async-done | bytes 9437200 | tf_op jit(solution)/shard_map/all_gather | solution.py:141
  140.1 35.6 %score.1 = f32[16,128]{1,0:T(8,128)} custom-call(bf16[4,9216,128]{2,1,0:T(8,128)(2,1)} %all-gather.5.cloned.1.call-done.x_ref, bf16[256,128,128]{2,1,0:T(8,128)(2,1)} %fusion.1.w_ref, bf16[272,256]{1,0:T(8,128)(2,1)} %pad_maximum_fusion.t_ref), custom_call_target="tpu_custom_call" | custom-call | tf_op jit(solution)/shard_map/score/pallas_call | solution.py:96
  (49 shorter events, 3.3 us)
Async XLA Ops:
  7.2 2.7 %copy-start = (s32[4,3]{1,0:T(4,128)S(1)}, s32[4,3]{1,0:T(4,128)}, u32[]{:S(2)}) copy-start(s32[4,3]{1,0:T(4,128)} %param.10) | copy-start | bytes 148
  7.2 87.7 %all-gather.7.cloned.1.call-start = ((), (), s32[]{:S(2)}) async-start(), calls=%async_computation.2 | async-start | bytes 3932160 | tf_op jit(solution)/shard_map/all_gather | solution.py:154
  19.5 24.5 %copy-start.1 = (s32[4,3]{1,0:T(4,128)S(1)}, s32[4,3]{1,0:T(4,128)}, u32[]{:S(2)}) copy-start(s32[4,3]{1,0:T(4,128)} %param.8) | copy-start | bytes 148
  19.5 24.6 %copy-start.2 = (bf16[4,3]{1,0:T(4,128)(2,1)S(1)}, bf16[4,3]{1,0:T(4,128)(2,1)}, u32[]{:S(2)}) copy-start(bf16[4,3]{1,0:T(4,128)(2,1)} %param.11) | copy-start | bytes 76
  19.6 24.6 %copy-start.3 = (s32[4]{0:T(128)S(1)}, s32[4]{0:T(128)}, u32[]{:S(2)}) copy-start(s32[4]{0:T(128)} %param.9) | copy-start | bytes 52
  43.2 96.9 %all-gather.5.cloned.1.call-start = ((), (), s32[]{:S(2)}) async-start(), calls=%async_computation.1 | async-start | bytes 11796480 | tf_op jit(solution)/shard_map/all_gather | solution.py:141
Sparse Core Ops, SparseCore 0:
  43.4 30.9 all-gather.6
  76.0 64.1 all-gather.4

commit v2 on v1

--- a/solution.py
+++ b/solution.py
@@ -25,15 +25,18 @@
     return jnp.concatenate([jnp.cos(phase_angle), -jnp.sin(phase_angle)]).astype(jnp.bfloat16)
 
 
-def score_kernel(dims, x_ref, w_ref, t_ref, out_ref, held):
+def score_kernel(dims, *refs):
     groups, each, shifts, angles, chunk, slots, kpad, scale = dims
+    x_refs = refs[:groups]
+    w_ref, t_ref, out_ref, held = refs[groups:]
+    stride = angles + 8
     rows = each * shifts
-    step = pl.program_id(1)
+    step = pl.program_id(0)
     first = step * chunk
 
     def quad(index, carry):
         blocks = [
-            x_ref[c, pl.ds(pl.multiple_of(index * 4 * rows, 16), 4 * rows), :] for c in range(groups)
+            ref[pl.ds(pl.multiple_of(index * 4 * rows, 16), 4 * rows), :] for ref in x_refs
         ]
         for part in range(4):
             start = part * rows // 16 * 16
@@ -48,13 +51,13 @@
             slot = 8 - (offset - skip)
             for c in range(groups):
                 value = prod[c * size + skip : c * size + skip + keep]
-                begin = (c * slots + slot) * angles + first + index * 4 + part
-                held[pl.ds(begin, keep, stride=angles), :] = value
+                begin = (c * slots + slot) * stride + first + index * 4 + part
+                held[pl.ds(begin, keep, stride=stride), :] = value
         return carry
 
     lax.fori_loop(0, chunk // 4, quad, 0, unroll=2)
 
-    @pl.when(step == pl.num_programs(1) - 1)
+    @pl.when(step == pl.num_programs(0) - 1)
     def _():
         table = t_ref[...]
         half = table.shape[0] // 2
@@ -67,7 +70,7 @@
                 for pair in range(0, each, 2):
                     cols = []
                     for i in (pair, pair + 1):
-                        at = pl.multiple_of((c * slots + 8 + s * each + i) * angles, angles)
+                        at = pl.multiple_of((c * slots + 8 + s * each + i) * stride, 8)
                         cols.append(held[pl.ds(at, angles), :].astype(jnp.bfloat16))
                     both = jnp.dot(table, jnp.concatenate(cols, axis=1), preferred_element_type=jnp.float32)
                     for h in range(2):
@@ -85,8 +88,7 @@
 
 
 def score(images, weights_of, table, each, shifts):
-    all_groups = images.shape[0]
-    groups = math.gcd(all_groups, 4)
+    groups = len(images)
     angles, width, parts = weights_of.shape
     rows = each * shifts
     chunk = 32
@@ -95,29 +97,34 @@
     dims = (groups, each, shifts, angles, chunk, slots, width // 2, scale)
     return pl.pallas_call(
         functools.partial(score_kernel, dims),
-        out_shape=jax.ShapeDtypeStruct((all_groups * each, width), jnp.float32),
-        grid=(all_groups // groups, angles // chunk),
+        out_shape=jax.ShapeDtypeStruct((groups * each, width), jnp.float32),
+        grid=(angles // chunk,),
         in_specs=[
-            pl.BlockSpec((groups, chunk * rows, parts), lambda b, g: (b, g, 0)),
-            pl.BlockSpec((chunk, width, parts), lambda b, g: (g, 0, 0)),
-            pl.BlockSpec(table.shape, lambda b, g: (0, 0)),
+            *[pl.BlockSpec((chunk * rows, parts), lambda g: (g, 0))] * groups,
+            pl.BlockSpec((chunk, width, parts), lambda g: (g, 0, 0)),
+            pl.BlockSpec(table.shape, lambda g: (0, 0)),
         ],
-        out_specs=pl.BlockSpec((groups * each, width), lambda b, g: (b, 0)),
-        scratch_shapes=[pltpu.VMEM((groups * slots * angles, width), jnp.float32)],
+        out_specs=pl.BlockSpec((groups * each, width), lambda g: (0, 0)),
+        scratch_shapes=[pltpu.VMEM((groups * slots * (angles + 8), width), jnp.float32)],
         compiler_params=pltpu.CompilerParams(vmem_limit_bytes=VMEM_LIMIT),
+        cost_estimate=pl.CostEstimate(
+            flops=groups * angles * 2**25, bytes_accessed=groups * angles * rows * parts * 2, transcendentals=0
+        ),
         name="score",
-    )(images, weights_of, table)
-
-
-def mean_kernel(block, own, x_ref, s_ref, d_ref, out_ref):
-    many = x_ref.shape[0]
-    parts = x_ref.shape[2]
+    )(*images, weights_of, table)
+
+
+def mean_kernel(block, own, *refs):
+    *x_refs, s_ref, d_ref, out_ref = refs
+    many = x_refs[0].shape[0]
+    parts = x_refs[0].shape[2]
     classes = d_ref.shape[0]
     weights = s_ref[...]
     scale = d_ref[...]
 
     def body(index, carry):
-        rows = x_ref[:, pl.ds(pl.multiple_of(index * block, 16), block), :].reshape(many * block, parts)
+        at = pl.ds(pl.multiple_of(index * block, 16), block)
+        rows = jnp.concatenate([ref[:, at, :].reshape(many * block, parts) for ref in x_refs], axis=0)
         sums = jnp.dot(weights, rows, preferred_element_type=jnp.float32)
         for part in range(4):
             value = sums[part * classes : (part + 1) * classes] / scale
@@ -127,10 +134,34 @@
     lax.fori_loop(0, own // 4, body, 0)
 
 
+def swap(value, axis, mask):
+    return lax.ppermute(value, axis, [(i, i ^ mask) for i in range(lax.axis_size(axis))])
+
+
+def reorder(value, order, axis):
+    value = jnp.moveaxis(value, axis, 0)
+    hit = order[:, None] == jnp.arange(value.shape[0], dtype=jnp.int32)[None, :]
+    hit = hit.reshape(hit.shape + (1,) * (value.ndim - 1))
+    return jnp.moveaxis(jnp.sum(jnp.where(hit, value[None], 0.0), axis=1), 0, axis)
+
+
+def gather_shards(value):
+    shards = {0: value}
+    bit = lax.axis_size("cls") // 2
+    while bit:
+        for mask in sorted(shards):
+            shards[mask | bit] = swap(shards[mask], "cls", bit)
+        bit //= 2
+    return [shards[mask] for mask in sorted(shards)]
+
+
 def on_device(particles, references, class_ids, counts, shift_ids, weights):
     dom_size = lax.axis_size("dom")
     cls_size = lax.axis_size("cls")
     cls_index = lax.axis_index("cls")
+    dom_index = lax.axis_index("dom")
+    cls_order = jnp.arange(cls_size, dtype=jnp.int32) ^ cls_index
+    dom_order = jnp.arange(dom_size, dtype=jnp.int32) ^ dom_index
     angles, class_count, parts = references.shape
     cycles = parts // 2
     each, shifts = particles.shape[1:3]
@@ -138,7 +169,7 @@
     own = angles // dom_size
 
     ordered = jnp.transpose(particles, (0, 2, 1, 3))
-    images = lax.all_gather(ordered.reshape(angles * shifts * each, parts), "cls", axis=0)
+    flat = ordered.reshape(angles * shifts * each, parts)
 
     valid = jnp.arange(length, dtype=jnp.int32)[None, :] < counts[:, None]
     kept = jnp.where(valid, weights.astype(jnp.float32), 0.0)
@@ -150,17 +181,37 @@
     for s in range(1, shifts):
         chosen = jnp.where(shift_of == s, ordered[:, s : s + 1], chosen)
     sent = chosen.reshape(dom_size, own * length * each, parts)
-    received = lax.all_to_all(sent, "dom", split_axis=0, concat_axis=0, tiled=True)
-    received = lax.all_gather(received, "cls", axis=0)
-    received = received.reshape(cls_size * dom_size, own * length * each, parts)
+    arrived = []
+    for mask in range(dom_size):
+        piece = lax.dynamic_index_in_dim(sent, dom_index ^ mask, 0, keepdims=True)
+        arrived.append(swap(piece, "dom", mask) if mask else piece)
+    received = gather_shards(jnp.concatenate(arrived, axis=0))
 
     kpad = up(class_count, 64)
     swapped = jnp.concatenate([-references[:, :, cycles:], references[:, :, :cycles]], axis=2)
     margin = ((0, 0), (0, kpad - class_count), (0, 0))
     stacked = jnp.concatenate([jnp.pad(references, margin), jnp.pad(swapped, margin)], axis=1)
-    best = score(images, stacked, half_table(angles), each, shifts)[:, :class_count]
+    table = half_table(angles)
+    bit, far = cls_size // 2, [flat]
+    while bit > 1:
+        far = far + [swap(shard, "cls", bit) for shard in far]
+        bit //= 2
+    best = [score([flat, swap(flat, "cls", 1)], stacked, table, each, shifts)]
+    rest = far[1:]
+    *rest, best[0] = lax.optimization_barrier((*rest, best[0]))
+    best = best + [score([shard, swap(shard, "cls", 1)], stacked, table, each, shifts) for shard in rest]
+    *received, best[-1] = lax.optimization_barrier((*received, best[-1]))
+    masks = [0]
+    bit = cls_size // 2
+    while bit > 1:
+        masks = masks + [mask | bit for mask in masks]
+        bit //= 2
+    best = [best[masks.index(mask)] for mask in sorted(masks)]
+    best = jnp.concatenate(best, axis=0)[:, :class_count].reshape(cls_size, each, class_count)
+    best = reorder(best, cls_order, 0).reshape(cls_size * each, class_count)
 
     listing = listing.reshape(dom_size, cls_size, 2, length * each).transpose(2, 1, 0, 3)
+    listing = reorder(reorder(listing, cls_order, 1), dom_order, 2)
     local = listing[0].reshape(-1, length * each) - (cls_index * class_count).astype(jnp.float32)
     kept_all = listing[1].reshape(-1, length * each)
     mine = local[None] == jnp.arange(class_count, dtype=jnp.int32).astype(jnp.float32)[:, None, None]
@@ -176,11 +227,11 @@
     means = pl.pallas_call(
         functools.partial(mean_kernel, block, own),
         out_shape=jax.ShapeDtypeStruct((kept_rows * own, parts), jnp.float32),
-        in_specs=[pl.BlockSpec(memory_space=pltpu.VMEM)] * 3,
+        in_specs=[pl.BlockSpec(memory_space=pltpu.VMEM)] * (cls_size + 2),
         out_specs=pl.BlockSpec(memory_space=pltpu.VMEM),
         compiler_params=pltpu.CompilerParams(vmem_limit_bytes=VMEM_LIMIT),
         name="means",
-    )(received, spread, jnp.broadcast_to(totals[:, None], (kept_rows, parts)))
+    )(*received, spread, jnp.broadcast_to(totals[:, None], (kept_rows, parts)))
     means = means.reshape(kept_rows, own, parts)[:class_count]
     return (best, jnp.transpose(means, (1, 0, 2)))
 

time: 184 us -> 159 us (0.86)
  blocking collectives: 57.2 us -> 32.3 us
  starting transfers between devices: 0.08 us -> 21.6 us
  waiting for transfers between devices: 36.9 us -> 21 us
  between operations: 14.4 us -> 1.2 us
  other arithmetic: 14.3 us -> 18.7 us
    all_gather x2 -> x0, waiting for transfers between devices: 36.2 us -> none  [the longest x1 36.2 us: on_device(): lax.all_gather(ordered.reshape(angles * shifts * each, parts), 'cls', axi...]
    all_to_all x1 -> x0, blocking collectives: 23.6 us -> none  [on_device(): lax.all_to_all(sent, 'dom', split_axis=0, concat_axis=0, tiled=True)]
    ppermute x0 -> x13, starting transfers between devices: none -> 21.6 us  [swap(): lax.ppermute(value, axis, [(i, i ^ mask) for i in range(lax.axis_size(axi...]
    ppermute x0 -> x13, waiting for transfers between devices: none -> 21 us  [swap(): lax.ppermute(value, axis, [(i, i ^ mask) for i in range(lax.axis_size(axi...]
    neg x1, other arithmetic: 1.53 us -> 4.68 us  [on_device(): -references[:, :, cycles:]]
    pallas_call x1 -> x2, Pallas kernels: 35.6 us -> 37.2 us  [score(): pl.pallas_call(functools.partial(score_kernel, dims), out_shape=jax.Shape...]
    unnamed x9 -> x29, local copies, waits for them, and re-layouts: 4.54 us -> 4.39 us
  transfers between devices with their start and end apart: 2 -> 13, of which waited for: 1 -> 3; matrix products, arithmetic and copies ran while one was open for 11% -> 21% of each run, Pallas kernels for 3% -> 24%
where the time goes in v2:
time: 159 us; the launch traced here: 156 us
  Pallas kernels  43.5 us (27%)
  blocking collectives  32.3 us (20%)
  starting transfers between devices  21.6 us (14%)
  waiting for transfers between devices  21 us (13%)
  other arithmetic  18.7 us (12%)
  local copies, waits for them, and re-layouts  17.9 us (11%)
    pallas_call x2, Pallas kernels, score(): pl.pallas_call(functools.partial(score_kernel, dims), out_shape=jax.Shape...  37.2 us
    all_gather x1, blocking collectives, on_device(): listing = lax.all_gather(packed, ('dom', 'cls'), axis=0)  32.3 us
    ppermute x13, starting transfers between devices, swap(): lax.ppermute(value, axis, [(i, i ^ mask) for i in range(lax.axis_size(axi...  21.6 us
    ppermute x13, waiting for transfers between devices, swap(): lax.ppermute(value, axis, [(i, i ^ mask) for i in range(lax.axis_size(axi...  21 us
    pallas_call x1, Pallas kernels, on_device(): pl.pallas_call(functools.partial(mean_kernel, block, own), out_shape=jax....  6.26 us
    neg x1, other arithmetic, on_device(): -references[:, :, cycles:]  4.68 us
    broadcast_in_dim x24, local copies, waits for them, and re-layouts, on_device(): chosen = jnp.where(shift_of == s, ordered[:, s:s + 1], chosen)  4.42 us
    unnamed x29, local copies, waits for them, and re-layouts  4.39 us
  transfers between devices with their start and end apart: 13, of which 3 were waited for; matrix products, arithmetic and copies ran while one was open for 21% of the time, Pallas kernels for 24%

profile of v2, /device:TPU:17, one launch (start us, length us, event | category | flops | bytes accessed | tf_op | source)
XLA Modules:
  0.0 156.1 jit_solution(6979106364249090689)
XLA Ops:
  0.6 0.7 collective-permute-start.1
  1.4 1.3 collective-permute-start
  2.6 2.7 %slice_bitcast_fusion = (bf16[256,4,128]{2,1,0:T(4,128)(2,1)S(1)}, bf16[256,4,128]{2,1,0:T(4,128)(2,1)S(1)}, bf16[256,4,128]{2,1,0:T(4,128)(2,1)S(1)}, bf16[256,...) fusion(bf16[256,9,4,128]{3,2,1,0:T(4,128)(2,1)} %bitcast.82), kind=kLoop, calls=%fused_computation.12 | loop fusion | bytes 4718592 | tf_op jit(solution)/shard_map/broadcast_in_dim | solution.py:180
  6.0 0.3 broadcast_in_dim.275
  11.0 4.2 %select_select_fusion = bf16[8,384,128]{2,1,0:T(8,128)(2,1)S(1)} fusion(bf16[8,384,128]{2,1,0:T(8,128)(2,1)S(1)} %bitcast.78, bf16[8,384,128]{2,1,0:T(8,128)(2,1)S(1)} %bitcast.79, bf16[8,384,128]{2,1,0:T(8,128)(2,1)S(1)} %bitcast.71, bf16[8,384,128]{2,1,0:T(8,128)(2,1)S(1)} %bitcast.72, bf16[8,384,128]{2,1,0:T(8,128)(2,1)S(1)} %bitcast.73, ...), kind=kLoop, calls=%fused_computation.9 | loop fusion | flops 3145728 | bytes 7888896 | tf_op jit(solution)/shard_map/jit(_where)/select_n | solution.py:182
  15.3 1.3 collective-permute-start.2
  16.6 1.3 collective-permute-start.3
  18.0 3.9 %copy.86 = bf16[256,50,128]{2,1,0:T(8,128)(2,1)} copy(bf16[256,50,128]{2,0,1:T(8,128)(2,1)S(1)} %copy-done.1) | data formatting | bytes 6553600 | tf_op args[1]
  22.0 0.6 cosine_convert_fusion
  22.9 0.7 pad_maximum_fusion.refs_3_
  23.7 4.7 %slice_negate_fusion = (bf16[256,50,64]{2,1,0:T(8,128)(2,1)S(1)}, bf16[256,50,64]{2,1,0:T(8,128)(2,1)S(1)}) fusion(bf16[256,50,128]{2,1,0:T(8,128)(2,1)} %copy.86), kind=kLoop, calls=%fused_computation.7 | loop fusion | flops 819200 | bytes 6553600 | tf_op jit(solution)/shard_map/neg | solution.py:191
  28.4 2.3 %fusion.4 = bf16[256,64,128]{2,1,0:T(8,128)(2,1)S(1)} fusion(bf16[256,50,64]{2,1,0:T(8,128)(2,1)S(1)} %get-tuple-element.17, bf16[256,50,64]{2,1,0:T(8,128)(2,1)S(1)} %get-tuple-element.16), kind=kLoop, calls=%fused_computation.6 | loop fusion | flops 14680064 | bytes 7471104 | tf_op jit(solution)/shard_map/concatenate | solution.py:191
  30.8 3.9 %fusion.1.refs_2_ = bf16[256,128,128]{2,1,0:T(8,128)(2,1)} fusion(bf16[256,50,128]{2,1,0:T(8,128)(2,1)S(1)} %copy-done, bf16[256,64,128]{2,1,0:T(8,128)(2,1)S(1)} %fusion.4), kind=kLoop, calls=%fused_computation.2 | loop fusion | flops 25165824 | bytes 15859712 | tf_op jit(solution)/shard_map/concatenate | solution.py:193
  34.7 18.6 %score.2 = f32[8,128]{1,0:T(8,128)} custom-call(bf16[9216,128]{1,0:T(8,128)(2,1)} %bitcast.83, bf16[9216,128]{1,0:T(8,128)(2,1)} %collective-permute-done.1.refs_1_, bf16[256,128,128]{2,1,0:T(8,128)(2,1)} %fusion.1.refs_2_, bf16[272,256]{1,0:T(8,128)(2,1)} %pad_maximum_fusion.refs_3_), custom_call_target="tpu_custom_call" | custom-call | flops 17179869184 | bytes 4718592 | tf_op jit(solution)/shard_map/score/pallas_call | solution.py:98
  53.3 1.2 collective-permute-done.refs_0_
  54.5 0.9 collective-permute-start.12
  55.4 32.3 %all-gather = f32[64,3,4]{2,1,0:T(4,128)S(1)} all-gather(f32[2,3,4]{2,1,0:T(4,128)S(1)} %pad_maximum_fusion.2), channel_id=2, replica_groups=mesh['dom'=8,'cls'=4] {'dom','cls'}, dimensions={0}, use_global_device_ids=true | all-gather | bytes 3168 | tf_op jit(solution)/shard_map/all_gather | solution.py:177
  88.1 7.1 %collective-permute-start.6 = (bf16[1,384,128]{2,1,0:T(8,128)(2,1)S(1)}, bf16[1,384,128]{2,1,0:T(8,128)(2,1)S(1)}, u32[]{:S(2)}, u32[]{:S(2)}) collective-permute-start(bf16[1,384,128]{2,1,0:T(8,128)(2,1)S(1)} %get-tuple-element.29), channel_id=1, source_target_pairs={{0,20},{4,16},{8,28},{12,24},{16,4},{20,0},{24,12},{28,8},{1,21},{... | collective-permute-start | bytes 294920 | tf_op jit(solution)/shard_map/ppermute | solution.py:138
  95.4 5.1 %collective-permute-start.8 = (bf16[1,384,128]{2,1,0:T(8,128)(2,1)S(1)}, bf16[1,384,128]{2,1,0:T(8,128)(2,1)S(1)}, u32[]{:S(2)}, u32[]{:S(2)}) collective-permute-start(bf16[1,384,128]{2,1,0:T(8,128)(2,1)S(1)} %get-tuple-element.27), channel_id=1, source_target_pairs={{0,28},{4,24},{8,20},{12,16},{16,12},{20,8},{24,4},{28,0},{1,29},{... | collective-permute-start | bytes 294920 | tf_op jit(solution)/shard_map/ppermute | solution.py:138
  100.6 6.5 %collective-permute-done.8 = bf16[1,384,128]{2,1,0:T(8,128)(2,1)S(1)} collective-permute-done((bf16[1,384,128]{2,1,0:T(8,128)(2,1)S(1)}, bf16[1,384,128]{2,1,0:T(8,128)(2,1)S(1)}, u32[]{:S(2)}, u32[]{:S(2)}) %collective-permute-start.8) | collective-permute-done | bytes 98336 | tf_op jit(solution)/shard_map/ppermute | solution.py:138
  107.1 0.6 collective-permute-start.10
  108.0 0.7 broadcast_multiply_fusion
  108.6 0.9 mul.56
  109.5 1.1 copy.102.refs_4_
  110.8 0.9 collective-permute-start.9
  111.7 13.3 %collective-permute-done.10.refs_2_ = bf16[8,384,128]{2,1,0:T(8,128)(2,1)} collective-permute-done((bf16[8,384,128]{2,1,0:T(8,128)(2,1)S(1)}, bf16[8,384,128]{2,1,0:T(8,128)(2,1)}, u32[]{:S(2)}, u32[]{:S(2)}) %collective-permute-start.10) | collective-permute-done | bytes 786464 | tf_op jit(solution)/shard_map/ppermute | solution.py:138
  125.0 2.2 %collective-permute-start.11 = (bf16[8,384,128]{2,1,0:T(8,128)(2,1)}, bf16[8,384,128]{2,1,0:T(8,128)(2,1)S(1)}, u32[]{:S(2)}, u32[]{:S(2)}) collective-permute-start(bf16[8,384,128]{2,1,0:T(8,128)(2,1)} %collective-permute-done.10.refs_2_), channel_id=1, source_target_pairs={{0,1},{1,0},{2,3},{3,2},{4,5},{5,4},{6,7},{7,6},{8,9},{9,8},{10,11... | collective-permute-start | bytes 2359304 | tf_op jit(solution)/shard_map/ppermute | solution.py:138
  127.2 18.6 %score.3 = f32[8,128]{1,0:T(8,128)} custom-call(bf16[9216,128]{1,0:T(8,128)(2,1)} %collective-permute-done.refs_0_, bf16[9216,128]{1,0:T(8,128)(2,1)} %collective-permute-done.12.refs_1_, bf16[256,128,128]{2,1,0:T(8,128)(2,1)} %fusion.1.refs_2_, bf16[272,256]{1,0:T(8,128)(2,1)} %pad_maximum_fusion.refs_3_), custom_call_target="tpu_custom_call" | custom-call | flops 17179869184 | bytes 4718592 | tf_op jit(solution)/shard_map/score/pallas_call | solution.py:98
  145.9 0.9 broadcast_in_dim.332.refs_5_
  147.0 6.3 %means.1 = f32[1792,128]{1,0:T(8,128)} custom-call(bf16[8,384,128]{2,1,0:T(8,128)(2,1)} %copy-done.2, bf16[8,384,128]{2,1,0:T(8,128)(2,1)} %copy-done.3, bf16[8,384,128]{2,1,0:T(8,128)(2,1)} %collective-permute-done.10.refs_2_, bf16[8,384,128]{2,1,0:T(8,128)(2,1)} %copy-done.4, bf16[224,1536]{1,0:T(8,128)(2,1)} %copy.102.refs_4_, ...), custom_call_target="tpu_custom_call" | custom-call | tf_op jit(solution)/shard_map/means/pallas_call | solution.py:227
  153.3 2.1 %slice.77 = f32[1600,128]{1,0:T(8,128)} slice(f32[1792,128]{1,0:T(8,128)} %means.1), slice={[0:1600], [0:128]} | slice | bytes 1638400 | tf_op jit(solution)/shard_map/slice | solution.py:235
  155.4 0.7 select_reduce_fusion.3
  (100 shorter events, 7.3 us)
Async XLA Ops:
  0.6 4.7 %copy-start.7 = (s32[4,3]{1,0:T(4,128)S(1)}, s32[4,3]{1,0:T(4,128)}, u32[]{:S(2)}) copy-start(s32[4,3]{1,0:T(4,128)} %param.10) | copy-start | bytes 148
  0.6 34.0 %collective-permute-start.1 = (bf16[9216,128]{1,0:T(8,128)(2,1)}, bf16[9216,128]{1,0:T(8,128)(2,1)}, u32[]{:S(2)}, u32[]{:S(2)}) collective-permute-start(bf16[9216,128]{1,0:T(8,128)(2,1)} %bitcast.80), channel_id=1, source_target_pairs={{0,1},{1,0},{2,3},{3,2},{4,5},{5,4},{6,7},{7,6},{8,9},{9,8},{10,11... | collective-permute-start | bytes 7077896 | tf_op jit(solution)/shard_map/ppermute | solution.py:138
  1.4 53.1 %collective-permute-start = (bf16[9216,128]{1,0:T(8,128)(2,1)}, bf16[9216,128]{1,0:T(8,128)(2,1)}, u32[]{:S(2)}, u32[]{:S(2)}) collective-permute-start(bf16[9216,128]{1,0:T(8,128)(2,1)} %bitcast.81), channel_id=1, source_target_pairs={{0,2},{1,3},{2,0},{3,1},{4,6},{5,7},{6,4},{7,5},{8,10},{9,11},{10,... | collective-permute-start | bytes 7077896 | tf_op jit(solution)/shard_map/ppermute | solution.py:138
  11.0 7.0 %copy-start.1 = (bf16[256,50,128]{2,0,1:T(8,128)(2,1)S(1)}, bf16[256,50,128]{2,0,1:T(8,128)(2,1)}, u32[]{:S(2)}) copy-start(bf16[256,50,128]{2,0,1:T(8,128)(2,1)} %param.7) | copy-start | bytes 9830404
  15.2 7.4 %copy-start.8 = (s32[4,3]{1,0:T(4,128)S(1)}, s32[4,3]{1,0:T(4,128)}, u32[]{:S(2)}) copy-start(s32[4,3]{1,0:T(4,128)} %param.8) | copy-start | bytes 148
  15.2 7.6 %copy-start.9 = (bf16[4,3]{1,0:T(4,128)(2,1)S(1)}, bf16[4,3]{1,0:T(4,128)(2,1)}, u32[]{:S(2)}) copy-start(bf16[4,3]{1,0:T(4,128)(2,1)} %param.11) | copy-start | bytes 76
  15.2 7.5 %copy-start.10 = (s32[4]{0:T(128)S(1)}, s32[4]{0:T(128)}, u32[]{:S(2)}) copy-start(s32[4]{0:T(128)} %param.9) | copy-start | bytes 52
  15.3 72.8 %collective-permute-start.2 = (bf16[1,384,128]{2,1,0:T(8,128)(2,1)S(1)}, bf16[1,384,128]{2,1,0:T(8,128)(2,1)S(1)}, u32[]{:S(2)}, u32[]{:S(2)}) collective-permute-start(bf16[1,384,128]{2,1,0:T(8,128)(2,1)S(1)} %get-tuple-element.33), channel_id=1, source_target_pairs={{0,4},{4,0},{8,12},{12,8},{16,20},{20,16},{24,28},{28,24},{1,5},{5... | collective-permute-start | bytes 294920 | tf_op jit(solution)/shard_map/ppermute | solution.py:138
  16.6 78.7 %collective-permute-start.3 = (bf16[1,384,128]{2,1,0:T(8,128)(2,1)S(1)}, bf16[1,384,128]{2,1,0:T(8,128)(2,1)S(1)}, u32[]{:S(2)}, u32[]{:S(2)}) collective-permute-start(bf16[1,384,128]{2,1,0:T(8,128)(2,1)S(1)} %get-tuple-element.32), channel_id=1, source_target_pairs={{0,8},{4,12},{8,0},{12,4},{16,24},{20,28},{24,16},{28,20},{1,9},{5... | collective-permute-start | bytes 294920 | tf_op jit(solution)/shard_map/ppermute | solution.py:138
  17.9 77.5 %collective-permute-start.4 = (bf16[1,384,128]{2,1,0:T(8,128)(2,1)S(1)}, bf16[1,384,128]{2,1,0:T(8,128)(2,1)S(1)}, u32[]{:S(2)}, u32[]{:S(2)}) collective-permute-start(bf16[1,384,128]{2,1,0:T(8,128)(2,1)S(1)} %get-tuple-element.31), channel_id=1, source_target_pairs={{0,12},{4,8},{8,4},{12,0},{16,28},{20,24},{24,20},{28,16},{1,13},{... | collective-permute-start | bytes 294920 | tf_op jit(solution)/shard_map/ppermute | solution.py:138
  28.4 2.3 %copy-start = (bf16[256,50,128]{2,1,0:T(8,128)(2,1)S(1)}, bf16[256,50,128]{2,1,0:T(8,128)(2,1)}, u32[]{:S(2)}) copy-start(bf16[256,50,128]{2,1,0:T(8,128)(2,1)} %copy.86) | copy-start | bytes 9830404
  34.7 65.9 %collective-permute-start.5 = (bf16[1,384,128]{2,1,0:T(8,128)(2,1)S(1)}, bf16[1,384,128]{2,1,0:T(8,128)(2,1)S(1)}, u32[]{:S(2)}, u32[]{:S(2)}) collective-permute-start(bf16[1,384,128]{2,1,0:T(8,128)(2,1)S(1)} %get-tuple-element.30), channel_id=1, source_target_pairs={{0,16},{4,20},{8,24},{12,28},{16,0},{20,4},{24,8},{28,12},{1,17},{... | collective-permute-start | bytes 294920 | tf_op jit(solution)/shard_map/ppermute | solution.py:138
  54.5 72.7 %collective-permute-start.12 = (bf16[9216,128]{1,0:T(8,128)(2,1)}, bf16[9216,128]{1,0:T(8,128)(2,1)}, u32[]{:S(2)}, u32[]{:S(2)}) collective-permute-start(bf16[9216,128]{1,0:T(8,128)(2,1)} %collective-permute-done.refs_0_), channel_id=1, source_target_pairs={{0,1},{1,0},{2,3},{3,2},{4,5},{5,4},{6,7},{7,6},{8,9},{9,8},{10,11... | collective-permute-start | bytes 7077896 | tf_op jit(solution)/shard_map/ppermute | solution.py:138
  88.1 12.4 %collective-permute-start.6 = (bf16[1,384,128]{2,1,0:T(8,128)(2,1)S(1)}, bf16[1,384,128]{2,1,0:T(8,128)(2,1)S(1)}, u32[]{:S(2)}, u32[]{:S(2)}) collective-permute-start(bf16[1,384,128]{2,1,0:T(8,128)(2,1)S(1)} %get-tuple-element.29), channel_id=1, source_target_pairs={{0,20},{4,16},{8,28},{12,24},{16,4},{20,0},{24,12},{28,8},{1,21},{... | collective-permute-start | bytes 294920 | tf_op jit(solution)/shard_map/ppermute | solution.py:138
  95.3 5.3 %collective-permute-start.7 = (bf16[1,384,128]{2,1,0:T(8,128)(2,1)S(1)}, bf16[1,384,128]{2,1,0:T(8,128)(2,1)S(1)}, u32[]{:S(2)}, u32[]{:S(2)}) collective-permute-start(bf16[1,384,128]{2,1,0:T(8,128)(2,1)S(1)} %get-tuple-element.28), channel_id=1, source_target_pairs={{0,24},{4,28},{8,16},{12,20},{16,8},{20,12},{24,0},{28,4},{1,25},{... | collective-permute-start | bytes 294920 | tf_op jit(solution)/shard_map/ppermute | solution.py:138
  95.4 11.7 %collective-permute-start.8 = (bf16[1,384,128]{2,1,0:T(8,128)(2,1)S(1)}, bf16[1,384,128]{2,1,0:T(8,128)(2,1)S(1)}, u32[]{:S(2)}, u32[]{:S(2)}) collective-permute-start(bf16[1,384,128]{2,1,0:T(8,128)(2,1)S(1)} %get-tuple-element.27), channel_id=1, source_target_pairs={{0,28},{4,24},{8,20},{12,16},{16,12},{20,8},{24,4},{28,0},{1,29},{... | collective-permute-start | bytes 294920 | tf_op jit(solution)/shard_map/ppermute | solution.py:138
  107.1 38.7 %copy-start.2 = (bf16[8,384,128]{2,1,0:T(8,128)(2,1)}, bf16[8,384,128]{2,1,0:T(8,128)(2,1)S(1)}, u32[]{:S(2)}) copy-start(bf16[8,384,128]{2,1,0:T(8,128)(2,1)S(1)} %constant_dynamic-update-slice_fusion.refs_0_) | copy-start | bytes 2359300
  107.1 17.9 %collective-permute-start.10 = (bf16[8,384,128]{2,1,0:T(8,128)(2,1)S(1)}, bf16[8,384,128]{2,1,0:T(8,128)(2,1)}, u32[]{:S(2)}, u32[]{:S(2)}) collective-permute-start(bf16[8,384,128]{2,1,0:T(8,128)(2,1)S(1)} %constant_dynamic-update-slice_fusion.refs_0_), channel_id=1, source_target_pairs={{0,2},{1,3},{2,0},{3,1},{4,6},{5,7},{6,4},{7,5},{8,10},{9,11},{10,... | collective-permute-start | bytes 2359304 | tf_op jit(solution)/shard_map/ppermute | solution.py:138
  110.8 35.0 %collective-permute-start.9 = (bf16[8,384,128]{2,1,0:T(8,128)(2,1)S(1)}, bf16[8,384,128]{2,1,0:T(8,128)(2,1)S(1)}, u32[]{:S(2)}, u32[]{:S(2)}) collective-permute-start(bf16[8,384,128]{2,1,0:T(8,128)(2,1)S(1)} %constant_dynamic-update-slice_fusion.refs_0_), channel_id=1, source_target_pairs={{0,1},{1,0},{2,3},{3,2},{4,5},{5,4},{6,7},{7,6},{8,9},{9,8},{10,11... | collective-permute-start | bytes 2359304 | tf_op jit(solution)/shard_map/ppermute | solution.py:138
  125.0 20.9 %collective-permute-start.11 = (bf16[8,384,128]{2,1,0:T(8,128)(2,1)}, bf16[8,384,128]{2,1,0:T(8,128)(2,1)S(1)}, u32[]{:S(2)}, u32[]{:S(2)}) collective-permute-start(bf16[8,384,128]{2,1,0:T(8,128)(2,1)} %collective-permute-done.10.refs_2_), channel_id=1, source_target_pairs={{0,1},{1,0},{2,3},{3,2},{4,5},{5,4},{6,7},{7,6},{8,9},{9,8},{10,11... | collective-permute-start | bytes 2359304 | tf_op jit(solution)/shard_map/ppermute | solution.py:138
  145.8 9.6 %copy-start.5 = (f32[8,128]{1,0:T(8,128)S(1)}, f32[8,128]{1,0:T(8,128)}, u32[]{:S(2)}) copy-start(f32[8,128]{1,0:T(8,128)} %score.2) | copy-start | bytes 12292
  145.8 9.6 %copy-start.6 = (f32[8,128]{1,0:T(8,128)S(1)}, f32[8,128]{1,0:T(8,128)}, u32[]{:S(2)}) copy-start(f32[8,128]{1,0:T(8,128)} %score.3) | copy-start | bytes 12292
  145.8 1.0 copy-start.3
  145.9 1.2 copy-start.4

commit v3 on v2

--- a/solution.py
+++ b/solution.py
@@ -118,16 +118,17 @@
     *x_refs, s_ref, d_ref, out_ref = refs
     many = x_refs[0].shape[0]
     parts = x_refs[0].shape[2]
-    classes = d_ref.shape[0]
+    classes = out_ref.shape[0] // own
+    pitch = d_ref.shape[0]
     weights = s_ref[...]
-    scale = d_ref[...]
+    scale = d_ref[:classes]
 
     def body(index, carry):
         at = pl.ds(pl.multiple_of(index * block, 16), block)
         rows = jnp.concatenate([ref[:, at, :].reshape(many * block, parts) for ref in x_refs], axis=0)
         sums = jnp.dot(weights, rows, preferred_element_type=jnp.float32)
         for part in range(4):
-            value = sums[part * classes : (part + 1) * classes] / scale
+            value = sums[part * pitch : part * pitch + classes] / scale
             out_ref[pl.ds(index * 4 + part, classes, stride=own), :] = value
         return carry
 
@@ -143,16 +144,6 @@
     hit = order[:, None] == jnp.arange(value.shape[0], dtype=jnp.int32)[None, :]
     hit = hit.reshape(hit.shape + (1,) * (value.ndim - 1))
     return jnp.moveaxis(jnp.sum(jnp.where(hit, value[None], 0.0), axis=1), 0, axis)
-
-
-def gather_shards(value):
-    shards = {0: value}
-    bit = lax.axis_size("cls") // 2
-    while bit:
-        for mask in sorted(shards):
-            shards[mask | bit] = swap(shards[mask], "cls", bit)
-        bit //= 2
-    return [shards[mask] for mask in sorted(shards)]
 
 
 def on_device(particles, references, class_ids, counts, shift_ids, weights):
@@ -161,7 +152,6 @@
     cls_index = lax.axis_index("cls")
     dom_index = lax.axis_index("dom")
     cls_order = jnp.arange(cls_size, dtype=jnp.int32) ^ cls_index
-    dom_order = jnp.arange(dom_size, dtype=jnp.int32) ^ dom_index
     angles, class_count, parts = references.shape
     cycles = parts // 2
     each, shifts = particles.shape[1:3]
@@ -172,20 +162,22 @@
     flat = ordered.reshape(angles * shifts * each, parts)
 
     valid = jnp.arange(length, dtype=jnp.int32)[None, :] < counts[:, None]
-    kept = jnp.where(valid, weights.astype(jnp.float32), 0.0)
-    packed = jnp.stack([class_ids.astype(jnp.float32).T, kept.T])
-    listing = lax.all_gather(packed, ("dom", "cls"), axis=0)
+    kept = jnp.where(valid, weights, jnp.zeros_like(weights)).T.reshape(1, length * each)
+    ids = class_ids.T.reshape(1, length * each)
+    packed = jnp.concatenate([kept, (ids // 32).astype(jnp.bfloat16), (ids % 32).astype(jnp.bfloat16)], axis=0)
+    packed = jnp.pad(packed, ((0, 16 - packed.shape[0]), (0, parts - length * each)))
 
     shift_of = shift_ids.T[None, :, :, None]
     chosen = jnp.broadcast_to(ordered[:, 0:1], (angles, length, each, parts))
     for s in range(1, shifts):
         chosen = jnp.where(shift_of == s, ordered[:, s : s + 1], chosen)
     sent = chosen.reshape(dom_size, own * length * each, parts)
+    sent = jnp.concatenate([sent, jnp.broadcast_to(packed[None], (dom_size, 16, parts))], axis=1)
     arrived = []
     for mask in range(dom_size):
         piece = lax.dynamic_index_in_dim(sent, dom_index ^ mask, 0, keepdims=True)
         arrived.append(swap(piece, "dom", mask) if mask else piece)
-    received = gather_shards(jnp.concatenate(arrived, axis=0))
+    received = jnp.concatenate(arrived, axis=0)
 
     kpad = up(class_count, 64)
     swapped = jnp.concatenate([-references[:, :, cycles:], references[:, :, :cycles]], axis=2)
@@ -196,9 +188,15 @@
     while bit > 1:
         far = far + [swap(shard, "cls", bit) for shard in far]
         bit //= 2
-    best = [score([flat, swap(flat, "cls", 1)], stacked, table, each, shifts)]
+    near, received, stacked, table = lax.optimization_barrier((swap(flat, "cls", 1), received, stacked, table))
+    best = [score([flat, near], stacked, table, each, shifts)]
+    bit, lists = cls_size // 2, [received]
+    while bit > 1:
+        lists = lists + [swap(listed, "cls", bit) for listed in lists]
+        bit //= 2
     rest = far[1:]
-    *rest, best[0] = lax.optimization_barrier((*rest, best[0]))
+    *rest, best[0], lists = lax.optimization_barrier((*rest, best[0], lists))
+    received = [entry for listed in lists for entry in (listed, swap(listed, "cls", 1))]
     best = best + [score([shard, swap(shard, "cls", 1)], stacked, table, each, shifts) for shard in rest]
     *received, best[-1] = lax.optimization_barrier((*received, best[-1]))
     masks = [0]
@@ -210,10 +208,10 @@
     best = jnp.concatenate(best, axis=0)[:, :class_count].reshape(cls_size, each, class_count)
     best = reorder(best, cls_order, 0).reshape(cls_size * each, class_count)
 
-    listing = listing.reshape(dom_size, cls_size, 2, length * each).transpose(2, 1, 0, 3)
-    listing = reorder(reorder(listing, cls_order, 1), dom_order, 2)
-    local = listing[0].reshape(-1, length * each) - (cls_index * class_count).astype(jnp.float32)
-    kept_all = listing[1].reshape(-1, length * each)
+    listing = jnp.concatenate([entry[:, own * length * each :][:, :3, : length * each] for entry in received])
+    listing = listing.astype(jnp.float32)
+    kept_all = listing[:, 0]
+    local = listing[:, 1] * 32.0 + listing[:, 2] - (cls_index * class_count).astype(jnp.float32)
     mine = local[None] == jnp.arange(class_count, dtype=jnp.int32).astype(jnp.float32)[:, None, None]
     picked = jnp.where(mine, kept_all[None], 0.0)
     totals = jnp.maximum(jnp.sum(picked, axis=(1, 2)), 1.0)
@@ -226,13 +224,13 @@
     spread = spread.reshape(4 * kept_rows, many * block)
     means = pl.pallas_call(
         functools.partial(mean_kernel, block, own),
-        out_shape=jax.ShapeDtypeStruct((kept_rows * own, parts), jnp.float32),
+        out_shape=jax.ShapeDtypeStruct((class_count * own, parts), jnp.float32),
         in_specs=[pl.BlockSpec(memory_space=pltpu.VMEM)] * (cls_size + 2),
         out_specs=pl.BlockSpec(memory_space=pltpu.VMEM),
         compiler_params=pltpu.CompilerParams(vmem_limit_bytes=VMEM_LIMIT),
         name="means",
     )(*received, spread, jnp.broadcast_to(totals[:, None], (kept_rows, parts)))
-    means = means.reshape(kept_rows, own, parts)[:class_count]
+    means = means.reshape(class_count, own, parts)
     return (best, jnp.transpose(means, (1, 0, 2)))
 
 

time: 159 us -> 117 us (0.74); the launches traced: 156 us -> 117 us
  blocking collectives: 32.3 us -> 0 us
  waiting for transfers between devices: 21 us -> 16.9 us
  starting transfers between devices: 21.6 us -> 18.4 us
  other arithmetic: 18.7 us -> 20.6 us
  local copies, waits for them, and re-layouts: 17.9 us -> 16.1 us
    all_gather x1 -> x0, blocking collectives: 32.3 us -> none  [on_device(): listing = lax.all_gather(packed, ('dom', 'cls'), axis=0)]
    ppermute x13, waiting for transfers between devices: 21 us -> 16.9 us  [swap(): lax.ppermute(value, axis, [(i, i ^ mask) for i in range(lax.axis_size(axi...]
    ppermute x13, starting transfers between devices: 21.6 us -> 18.4 us  [swap(): lax.ppermute(value, axis, [(i, i ^ mask) for i in range(lax.axis_size(axi...]
    concatenate x1, other arithmetic: 2.31 us -> 4.52 us  [on_device(): jnp.concatenate([-references[:, :, cycles:], references[:, :, :cycles]],...]
    slice x1 -> x8, local copies, waits for them, and re-layouts: 2.09 us -> 0.44 us  [on_device(): entry[:, own * length * each:][:, :3, :length * each]]
    unnamed x29 -> x31, local copies, waits for them, and re-layouts: 4.39 us -> 4.22 us
  transfers between devices with their start and end apart: 13 -> 13, of which waited for: 3 -> 5; matrix products, arithmetic and copies ran while one was open for 21% -> 27% of each run, Pallas kernels for 24% -> 32%
where the time goes in v3:
time: 117 us
  Pallas kernels  43.4 us (37%)
  other arithmetic  20.6 us (18%)
  starting transfers between devices  18.4 us (16%)
  waiting for transfers between devices  16.9 us (14%)
  local copies, waits for them, and re-layouts  16.1 us (14%)
    pallas_call x2, Pallas kernels, score(): pl.pallas_call(functools.partial(score_kernel, dims), out_shape=jax.Shape...  37.2 us
    ppermute x13, starting transfers between devices, swap(): lax.ppermute(value, axis, [(i, i ^ mask) for i in range(lax.axis_size(axi...  18.4 us
    ppermute x13, waiting for transfers between devices, swap(): lax.ppermute(value, axis, [(i, i ^ mask) for i in range(lax.axis_size(axi...  16.9 us
    pallas_call x1, Pallas kernels, on_device(): pl.pallas_call(functools.partial(mean_kernel, block, own), out_shape=jax....  6.18 us
    neg x1, other arithmetic, on_device(): -references[:, :, cycles:]  4.54 us
    concatenate x1, other arithmetic, on_device(): jnp.concatenate([-references[:, :, cycles:], references[:, :, :cycles]],...  4.52 us
    broadcast_in_dim x24, local copies, waits for them, and re-layouts, on_device(): chosen = jnp.where(shift_of == s, ordered[:, s:s + 1], chosen)  4.42 us
    unnamed x31, local copies, waits for them, and re-layouts  4.22 us
  transfers between devices with their start and end apart: 13, of which 5 were waited for; matrix products, arithmetic and copies ran while one was open for 27% of the time, Pallas kernels for 32%

profile of v3, /device:TPU:17, one launch (start us, length us, event | category | flops | bytes accessed | tf_op | source)
XLA Modules:
  0.0 116.6 jit_solution(5231024330996359053)
XLA Ops:
  0.7 0.7 collective-permute-start.1
  1.4 1.3 %collective-permute-start = (bf16[9216,128]{1,0:T(8,128)(2,1)}, bf16[9216,128]{1,0:T(8,128)(2,1)}, u32[]{:S(2)}, u32[]{:S(2)}) collective-permute-start(bf16[9216,128]{1,0:T(8,128)(2,1)} %bitcast.70), channel_id=1, source_target_pairs={{0,2},{1,3},{2,0},{3,1},{4,6},{5,7},{6,4},{7,5},{8,10},{9,11},{10,... | collective-permute-start | bytes 7077896 | tf_op jit(solution)/shard_map/ppermute | solution.py:139
  2.7 2.7 %slice_bitcast_fusion = (bf16[256,4,128]{2,1,0:T(4,128)(2,1)S(1)}, bf16[256,4,128]{2,1,0:T(4,128)(2,1)S(1)}, bf16[256,4,128]{2,1,0:T(4,128)(2,1)S(1)}, bf16[256,...) fusion(bf16[256,9,4,128]{3,2,1,0:T(4,128)(2,1)} %bitcast.71), kind=kLoop, calls=%fused_computation.20 | loop fusion | bytes 4718592 | tf_op jit(solution)/shard_map/broadcast_in_dim | solution.py:171
  5.5 0.3 broadcast_in_dim.224
  8.8 0.3 broadcast_in_dim.266
  11.5 4.2 %select_select_fusion = bf16[8,384,128]{2,1,0:T(8,128)(2,1)S(1)} fusion(bf16[8,384,128]{2,1,0:T(8,128)(2,1)S(1)} %bitcast.67, bf16[8,384,128]{2,1,0:T(8,128)(2,1)S(1)} %bitcast.68, bf16[8,384,128]{2,1,0:T(8,128)(2,1)S(1)} %bitcast.60, bf16[8,384,128]{2,1,0:T(8,128)(2,1)S(1)} %bitcast.61, bf16[8,384,128]{2,1,0:T(8,128)(2,1)S(1)} %bitcast.62, ...), kind=kLoop, calls=%fused_computation.17 | loop fusion | flops 3145728 | bytes 7888896 | tf_op jit(solution)/shard_map/jit(_where)/select_n | solution.py:173
  15.7 1.3 %collective-permute-start.2 = (bf16[1,400,128]{2,1,0:T(8,128)(2,1)S(1)}, bf16[1,400,128]{2,1,0:T(8,128)(2,1)S(1)}, u32[]{:S(2)}, u32[]{:S(2)}) collective-permute-start(bf16[1,400,128]{2,1,0:T(8,128)(2,1)S(1)} %get-tuple-element.41), channel_id=1, source_target_pairs={{0,4},{4,0},{8,12},{12,8},{16,20},{20,16},{24,28},{28,24},{1,5},{5... | collective-permute-start | bytes 307208 | tf_op jit(solution)/shard_map/ppermute | solution.py:139
  17.0 1.3 %collective-permute-start.3 = (bf16[1,400,128]{2,1,0:T(8,128)(2,1)S(1)}, bf16[1,400,128]{2,1,0:T(8,128)(2,1)S(1)}, u32[]{:S(2)}, u32[]{:S(2)}) collective-permute-start(bf16[1,400,128]{2,1,0:T(8,128)(2,1)S(1)} %get-tuple-element.42), channel_id=1, source_target_pairs={{0,8},{4,12},{8,0},{12,4},{16,24},{20,28},{24,16},{28,20},{1,9},{5... | collective-permute-start | bytes 307208 | tf_op jit(solution)/shard_map/ppermute | solution.py:139
  18.5 4.1 %copy.65 = bf16[256,50,128]{2,1,0:T(8,128)(2,1)S(1)} copy(bf16[256,50,128]{2,0,1:T(8,128)(2,1)} %param.7) | data formatting | bytes 6553600 | tf_op args[1]
  22.5 4.5 %slice_negate_fusion = (bf16[256,50,64]{2,1,0:T(8,128)(2,1)}, bf16[256,50,64]{2,1,0:T(8,128)(2,1)}) fusion(bf16[256,50,128]{2,1,0:T(8,128)(2,1)S(1)} %copy.65), kind=kLoop, calls=%fused_computation.7 | loop fusion | flops 819200 | bytes 6553600 | tf_op jit(solution)/shard_map/neg | solution.py:183
  27.1 0.6 cosine_convert_fusion
  27.8 4.5 %fusion.4 = bf16[256,64,128]{2,1,0:T(8,128)(2,1)S(1)} fusion(bf16[256,50,64]{2,1,0:T(8,128)(2,1)} %get-tuple-element.29, bf16[256,50,64]{2,1,0:T(8,128)(2,1)} %get-tuple-element.28), kind=kLoop, calls=%fused_computation.6 | loop fusion | flops 14680064 | bytes 7471104 | tf_op jit(solution)/shard_map/concatenate | solution.py:183
  32.3 3.9 %fusion.1.refs_2_ = bf16[256,128,128]{2,1,0:T(8,128)(2,1)} fusion(bf16[256,50,128]{2,1,0:T(8,128)(2,1)S(1)} %copy-done.1, bf16[256,64,128]{2,1,0:T(8,128)(2,1)S(1)} %fusion.4), kind=kLoop, calls=%fused_computation.2 | loop fusion | flops 25165824 | bytes 15859712 | tf_op jit(solution)/shard_map/concatenate | solution.py:185
  36.2 0.7 pad_maximum_fusion.refs_3_
  37.0 3.3 %collective-permute-start.6 = (bf16[1,400,128]{2,1,0:T(8,128)(2,1)S(1)}, bf16[1,400,128]{2,1,0:T(8,128)(2,1)S(1)}, u32[]{:S(2)}, u32[]{:S(2)}) collective-permute-start(bf16[1,400,128]{2,1,0:T(8,128)(2,1)S(1)} %get-tuple-element.46), channel_id=1, source_target_pairs={{0,20},{4,16},{8,28},{12,24},{16,4},{20,0},{24,12},{28,8},{1,21},{... | collective-permute-start | bytes 307208 | tf_op jit(solution)/shard_map/ppermute | solution.py:139
  40.6 0.8 collective-permute-done.5
  41.4 8.0 %collective-permute-start.8 = (bf16[1,400,128]{2,1,0:T(8,128)(2,1)S(1)}, bf16[1,400,128]{2,1,0:T(8,128)(2,1)S(1)}, u32[]{:S(2)}, u32[]{:S(2)}) collective-permute-start(bf16[1,400,128]{2,1,0:T(8,128)(2,1)S(1)} %get-tuple-element.39), channel_id=1, source_target_pairs={{0,28},{4,24},{8,20},{12,16},{16,12},{20,8},{24,4},{28,0},{1,29},{... | collective-permute-start | bytes 307208 | tf_op jit(solution)/shard_map/ppermute | solution.py:139
  49.5 4.2 %collective-permute-done.7 = bf16[1,400,128]{2,1,0:T(8,128)(2,1)S(1)} collective-permute-done((bf16[1,400,128]{2,1,0:T(8,128)(2,1)S(1)}, bf16[1,400,128]{2,1,0:T(8,128)(2,1)S(1)}, u32[]{:S(2)}, u32[]{:S(2)}) %collective-permute-start.7) | collective-permute-done | bytes 102432 | tf_op jit(solution)/shard_map/ppermute | solution.py:139
  53.7 5.2 %collective-permute-done.8 = bf16[1,400,128]{2,1,0:T(8,128)(2,1)S(1)} collective-permute-done((bf16[1,400,128]{2,1,0:T(8,128)(2,1)S(1)}, bf16[1,400,128]{2,1,0:T(8,128)(2,1)S(1)}, u32[]{:S(2)}, u32[]{:S(2)}) %collective-permute-start.8) | collective-permute-done | bytes 102432 | tf_op jit(solution)/shard_map/ppermute | solution.py:139
  59.0 0.3 collective-permute-start.9
  59.2 18.6 %score.2 = f32[8,128]{1,0:T(8,128)} custom-call(bf16[9216,128]{1,0:T(8,128)(2,1)} %bitcast.72, bf16[9216,128]{1,0:T(8,128)(2,1)} %collective-permute-done.1.refs_1_, bf16[256,128,128]{2,1,0:T(8,128)(2,1)} %fusion.1.refs_2_, bf16[272,256]{1,0:T(8,128)(2,1)} %pad_maximum_fusion.refs_3_), custom_call_target="tpu_custom_call" | custom-call | flops 17179869184 | bytes 4718592 | tf_op jit(solution)/shard_map/score/pallas_call | solution.py:98
  77.9 0.5 collective-permute-done.9.refs_2_
  78.3 1.3 %collective-permute-start.12 = (bf16[9216,128]{1,0:T(8,128)(2,1)}, bf16[9216,128]{1,0:T(8,128)(2,1)}, u32[]{:S(2)}, u32[]{:S(2)}) collective-permute-start(bf16[9216,128]{1,0:T(8,128)(2,1)} %collective-permute-done.refs_0_), channel_id=1, source_target_pairs={{0,1},{1,0},{2,3},{3,2},{4,5},{5,4},{6,7},{7,6},{8,9},{9,8},{10,11... | collective-permute-start | bytes 7077896 | tf_op jit(solution)/shard_map/ppermute | solution.py:139
  79.8 0.5 collective-permute-start.11
  80.3 6.1 %collective-permute-done.12.refs_1_ = bf16[9216,128]{1,0:T(8,128)(2,1)} collective-permute-done((bf16[9216,128]{1,0:T(8,128)(2,1)}, bf16[9216,128]{1,0:T(8,128)(2,1)}, u32[]{:S(2)}, u32[]{:S(2)}) %collective-permute-start.12) | collective-permute-done | bytes 2359328 | tf_op jit(solution)/shard_map/ppermute | solution.py:139
  86.4 18.6 %score.3 = f32[8,128]{1,0:T(8,128)} custom-call(bf16[9216,128]{1,0:T(8,128)(2,1)} %collective-permute-done.refs_0_, bf16[9216,128]{1,0:T(8,128)(2,1)} %collective-permute-done.12.refs_1_, bf16[256,128,128]{2,1,0:T(8,128)(2,1)} %fusion.1.refs_2_, bf16[272,256]{1,0:T(8,128)(2,1)} %pad_maximum_fusion.refs_3_), custom_call_target="tpu_custom_call" | custom-call | flops 17179869184 | bytes 4718592 | tf_op jit(solution)/shard_map/score/pallas_call | solution.py:98
  106.3 0.7 broadcast_multiply_fusion
  107.0 0.9 mul.69
  107.9 1.1 copy.74.refs_4_
  109.0 0.7 broadcast_in_dim.282.refs_5_
  109.7 6.2 %means.1 = f32[1600,128]{1,0:T(8,128)} custom-call(bf16[8,400,128]{2,1,0:T(8,128)(2,1)} %copy-done.2, bf16[8,400,128]{2,1,0:T(8,128)(2,1)} %copy-done.4, bf16[8,400,128]{2,1,0:T(8,128)(2,1)} %copy-done.3, bf16[8,400,128]{2,1,0:T(8,128)(2,1)} %copy-done.5, bf16[224,1536]{1,0:T(8,128)(2,1)} %copy.74.refs_4_, f32[56,128]{1,0:T(8,128)} %broadcast_in_dim.282.refs_5_), custom_call_target="tpu_custom_call" | custom-call | tf_op jit(solution)/shard_map/means/pallas_call | solution.py:225
  115.9 0.7 select_reduce_fusion.1
  (108 shorter events, 7.4 us)
Async XLA Ops:
  0.6 4.7 %copy-start.8 = (s32[4,3]{1,0:T(4,128)S(1)}, s32[4,3]{1,0:T(4,128)}, u32[]{:S(2)}) copy-start(s32[4,3]{1,0:T(4,128)} %param.10) | copy-start | bytes 148
  0.6 8.4 %copy-start.9 = (s32[4,3]{1,0:T(4,128)S(1)}, s32[4,3]{1,0:T(4,128)}, u32[]{:S(2)}) copy-start(s32[4,3]{1,0:T(4,128)} %param.8) | copy-start | bytes 148
  0.7 8.6 %copy-start.10 = (bf16[4,3]{1,0:T(4,128)(2,1)S(1)}, bf16[4,3]{1,0:T(4,128)(2,1)}, u32[]{:S(2)}) copy-start(bf16[4,3]{1,0:T(4,128)(2,1)} %param.11) | copy-start | bytes 76
  0.7 8.6 %copy-start.11 = (s32[4]{0:T(128)S(1)}, s32[4]{0:T(128)}, u32[]{:S(2)}) copy-start(s32[4]{0:T(128)} %param.9) | copy-start | bytes 52
  0.7 58.3 %collective-permute-start.1 = (bf16[9216,128]{1,0:T(8,128)(2,1)}, bf16[9216,128]{1,0:T(8,128)(2,1)}, u32[]{:S(2)}, u32[]{:S(2)}) collective-permute-start(bf16[9216,128]{1,0:T(8,128)(2,1)} %bitcast.69), channel_id=1, source_target_pairs={{0,1},{1,0},{2,3},{3,2},{4,5},{5,4},{6,7},{7,6},{8,9},{9,8},{10,11... | collective-permute-start | bytes 7077896 | tf_op jit(solution)/shard_map/ppermute | solution.py:139
  1.4 76.4 %collective-permute-start = (bf16[9216,128]{1,0:T(8,128)(2,1)}, bf16[9216,128]{1,0:T(8,128)(2,1)}, u32[]{:S(2)}, u32[]{:S(2)}) collective-permute-start(bf16[9216,128]{1,0:T(8,128)(2,1)} %bitcast.70), channel_id=1, source_target_pairs={{0,2},{1,3},{2,0},{3,1},{4,6},{5,7},{6,4},{7,5},{8,10},{9,11},{10,... | collective-permute-start | bytes 7077896 | tf_op jit(solution)/shard_map/ppermute | solution.py:139
  15.7 21.2 %collective-permute-start.2 = (bf16[1,400,128]{2,1,0:T(8,128)(2,1)S(1)}, bf16[1,400,128]{2,1,0:T(8,128)(2,1)S(1)}, u32[]{:S(2)}, u32[]{:S(2)}) collective-permute-start(bf16[1,400,128]{2,1,0:T(8,128)(2,1)S(1)} %get-tuple-element.41), channel_id=1, source_target_pairs={{0,4},{4,0},{8,12},{12,8},{16,20},{20,16},{24,28},{28,24},{1,5},{5... | collective-permute-start | bytes 307208 | tf_op jit(solution)/shard_map/ppermute | solution.py:139
  17.0 20.0 %collective-permute-start.3 = (bf16[1,400,128]{2,1,0:T(8,128)(2,1)S(1)}, bf16[1,400,128]{2,1,0:T(8,128)(2,1)S(1)}, u32[]{:S(2)}, u32[]{:S(2)}) collective-permute-start(bf16[1,400,128]{2,1,0:T(8,128)(2,1)S(1)} %get-tuple-element.42), channel_id=1, source_target_pairs={{0,8},{4,12},{8,0},{12,4},{16,24},{20,28},{24,16},{28,20},{1,9},{5... | collective-permute-start | bytes 307208 | tf_op jit(solution)/shard_map/ppermute | solution.py:139
  18.3 22.0 %collective-permute-start.4 = (bf16[1,400,128]{2,1,0:T(8,128)(2,1)S(1)}, bf16[1,400,128]{2,1,0:T(8,128)(2,1)S(1)}, u32[]{:S(2)}, u32[]{:S(2)}) collective-permute-start(bf16[1,400,128]{2,1,0:T(8,128)(2,1)S(1)} %get-tuple-element.43), channel_id=1, source_target_pairs={{0,12},{4,8},{8,4},{12,0},{16,28},{20,24},{24,20},{28,16},{1,13},{... | collective-permute-start | bytes 307208 | tf_op jit(solution)/shard_map/ppermute | solution.py:139
  22.5 4.5 %copy-start = (bf16[256,50,128]{2,1,0:T(8,128)(2,1)}, bf16[256,50,128]{2,1,0:T(8,128)(2,1)S(1)}, u32[]{:S(2)}) copy-start(bf16[256,50,128]{2,1,0:T(8,128)(2,1)S(1)} %copy.65) | copy-start | bytes 9830404
  27.8 4.5 %copy-start.1 = (bf16[256,50,128]{2,1,0:T(8,128)(2,1)S(1)}, bf16[256,50,128]{2,1,0:T(8,128)(2,1)}, u32[]{:S(2)}) copy-start(bf16[256,50,128]{2,1,0:T(8,128)(2,1)} %copy-done) | copy-start | bytes 9830404
  36.9 4.5 %collective-permute-start.5 = (bf16[1,400,128]{2,1,0:T(8,128)(2,1)S(1)}, bf16[1,400,128]{2,1,0:T(8,128)(2,1)S(1)}, u32[]{:S(2)}, u32[]{:S(2)}) collective-permute-start(bf16[1,400,128]{2,1,0:T(8,128)(2,1)S(1)} %get-tuple-element.44), channel_id=1, source_target_pairs={{0,16},{4,20},{8,24},{12,28},{16,0},{20,4},{24,8},{28,12},{1,17},{... | collective-permute-start | bytes 307208 | tf_op jit(solution)/shard_map/ppermute | solution.py:139
  37.0 12.4 %collective-permute-start.6 = (bf16[1,400,128]{2,1,0:T(8,128)(2,1)S(1)}, bf16[1,400,128]{2,1,0:T(8,128)(2,1)S(1)}, u32[]{:S(2)}, u32[]{:S(2)}) collective-permute-start(bf16[1,400,128]{2,1,0:T(8,128)(2,1)S(1)} %get-tuple-element.46), channel_id=1, source_target_pairs={{0,20},{4,16},{8,28},{12,24},{16,4},{20,0},{24,12},{28,8},{1,21},{... | collective-permute-start | bytes 307208 | tf_op jit(solution)/shard_map/ppermute | solution.py:139
  40.3 13.4 %collective-permute-start.7 = (bf16[1,400,128]{2,1,0:T(8,128)(2,1)S(1)}, bf16[1,400,128]{2,1,0:T(8,128)(2,1)S(1)}, u32[]{:S(2)}, u32[]{:S(2)}) collective-permute-start(bf16[1,400,128]{2,1,0:T(8,128)(2,1)S(1)} %get-tuple-element.45), channel_id=1, source_target_pairs={{0,24},{4,28},{8,16},{12,20},{16,8},{20,12},{24,0},{28,4},{1,25},{... | collective-permute-start | bytes 307208 | tf_op jit(solution)/shard_map/ppermute | solution.py:139
  41.4 17.5 %collective-permute-start.8 = (bf16[1,400,128]{2,1,0:T(8,128)(2,1)S(1)}, bf16[1,400,128]{2,1,0:T(8,128)(2,1)S(1)}, u32[]{:S(2)}, u32[]{:S(2)}) collective-permute-start(bf16[1,400,128]{2,1,0:T(8,128)(2,1)S(1)} %get-tuple-element.39), channel_id=1, source_target_pairs={{0,28},{4,24},{8,20},{12,16},{16,12},{20,8},{24,4},{28,0},{1,29},{... | collective-permute-start | bytes 307208 | tf_op jit(solution)/shard_map/ppermute | solution.py:139
  58.9 46.1 %copy-start.2 = (bf16[8,400,128]{2,1,0:T(8,128)(2,1)}, bf16[8,400,128]{2,1,0:T(8,128)(2,1)S(1)}, u32[]{:S(2)}) copy-start(bf16[8,400,128]{2,1,0:T(8,128)(2,1)S(1)} %constant_dynamic-update-slice_fusion.refs_0_) | copy-start | bytes 2457604
  59.0 19.4 %collective-permute-start.9 = (bf16[8,400,128]{2,1,0:T(8,128)(2,1)S(1)}, bf16[8,400,128]{2,1,0:T(8,128)(2,1)S(1)}, u32[]{:S(2)}, u32[]{:S(2)}) collective-permute-start(bf16[8,400,128]{2,1,0:T(8,128)(2,1)S(1)} %constant_dynamic-update-slice_fusion.refs_0_), channel_id=1, source_target_pairs={{0,2},{1,3},{2,0},{3,1},{4,6},{5,7},{6,4},{7,5},{8,10},{9,11},{10,... | collective-permute-start | bytes 2457608 | tf_op jit(solution)/shard_map/ppermute | solution.py:139
  78.3 27.0 %copy-start.3 = (bf16[8,400,128]{2,1,0:T(8,128)(2,1)}, bf16[8,400,128]{2,1,0:T(8,128)(2,1)S(1)}, u32[]{:S(2)}) copy-start(bf16[8,400,128]{2,1,0:T(8,128)(2,1)S(1)} %collective-permute-done.9.refs_2_) | copy-start | bytes 2457604
  78.3 8.1 %collective-permute-start.12 = (bf16[9216,128]{1,0:T(8,128)(2,1)}, bf16[9216,128]{1,0:T(8,128)(2,1)}, u32[]{:S(2)}, u32[]{:S(2)}) collective-permute-start(bf16[9216,128]{1,0:T(8,128)(2,1)} %collective-permute-done.refs_0_), channel_id=1, source_target_pairs={{0,1},{1,0},{2,3},{3,2},{4,5},{5,4},{6,7},{7,6},{8,9},{9,8},{10,11... | collective-permute-start | bytes 7077896 | tf_op jit(solution)/shard_map/ppermute | solution.py:139
  79.8 25.3 %collective-permute-start.10 = (bf16[8,400,128]{2,1,0:T(8,128)(2,1)S(1)}, bf16[8,400,128]{2,1,0:T(8,128)(2,1)S(1)}, u32[]{:S(2)}, u32[]{:S(2)}) collective-permute-start(bf16[8,400,128]{2,1,0:T(8,128)(2,1)S(1)} %constant_dynamic-update-slice_fusion.refs_0_), channel_id=1, source_target_pairs={{0,1},{1,0},{2,3},{3,2},{4,5},{5,4},{6,7},{7,6},{8,9},{9,8},{10,11... | collective-permute-start | bytes 2457608 | tf_op jit(solution)/shard_map/ppermute | solution.py:139
  79.8 25.2 %collective-permute-start.11 = (bf16[8,400,128]{2,1,0:T(8,128)(2,1)S(1)}, bf16[8,400,128]{2,1,0:T(8,128)(2,1)S(1)}, u32[]{:S(2)}, u32[]{:S(2)}) collective-permute-start(bf16[8,400,128]{2,1,0:T(8,128)(2,1)S(1)} %collective-permute-done.9.refs_2_), channel_id=1, source_target_pairs={{0,1},{1,0},{2,3},{3,2},{4,5},{5,4},{6,7},{7,6},{8,9},{9,8},{10,11... | collective-permute-start | bytes 2457608 | tf_op jit(solution)/shard_map/ppermute | solution.py:139
  105.0 1.2 %copy-start.4 = (bf16[8,400,128]{2,1,0:T(8,128)(2,1)}, bf16[8,400,128]{2,1,0:T(8,128)(2,1)S(1)}, u32[]{:S(2)}) copy-start(bf16[8,400,128]{2,1,0:T(8,128)(2,1)S(1)} %collective-permute-done.10.refs_1_) | copy-start | bytes 2457604
  105.0 4.6 %copy-start.5 = (bf16[8,400,128]{2,1,0:T(8,128)(2,1)}, bf16[8,400,128]{2,1,0:T(8,128)(2,1)S(1)}, u32[]{:S(2)}) copy-start(bf16[8,400,128]{2,1,0:T(8,128)(2,1)S(1)} %collective-permute-done.11.refs_3_) | copy-start | bytes 2457604
  107.0 8.9 %copy-start.6 = (f32[8,128]{1,0:T(8,128)S(1)}, f32[8,128]{1,0:T(8,128)}, u32[]{:S(2)}) copy-start(f32[8,128]{1,0:T(8,128)} %score.2) | copy-start | bytes 12292
  107.0 8.9 %copy-start.7 = (f32[8,128]{1,0:T(8,128)S(1)}, f32[8,128]{1,0:T(8,128)}, u32[]{:S(2)}) copy-start(f32[8,128]{1,0:T(8,128)} %score.3) | copy-start | bytes 12292
